TPU v7x, 32 devices: a whole 2x2x4 slice. The times are simulated.
32 devices in a mesh: sec: 4 (over x, core), fsdp: 8 (over z, y).
Axes of the slice: x: 2, y: 2, z: 4, core: 2. Of those that a mesh axis runs over, the one named last changes fastest.
Arguments:
- tokens: bfloat16 [4096, 6144], P('fsdp', 'sec'), may hold values from -6 to 6
- grad_out: bfloat16 [4096, 6144], P('fsdp', 'sec'), may hold values from -6 to 6
- gain: float32 [6144], P('sec'), may hold values from 0.1 to 7
- qkv_weight: bfloat16 [6144, 384], P(('sec', 'fsdp')), may hold values from -0.078125 to 0.078125
- out_weight: bfloat16 [128, 6144], P(None, ('sec', 'fsdp')), may hold values from -0.5 to 0.5
Outputs:
- grad_tokens: bfloat16 [4096, 6144], P('fsdp', 'sec')
- grad_qkv: float32 [6144, 384], P(('sec', 'fsdp'))
- grad_outw: float32 [128, 6144], P(None, ('sec', 'fsdp'))
- grad_gain: float32 [6144], P(('sec', 'fsdp'))
All inputs are finite; a program needn't handle non-finite values.
Results may differ from a plain program's by a relative error of at most 0.012.
The roundings to bfloat16 on the way count: a program that leaves them out, or rounds other values in their place, can miss the bound.
Values may be sent and summed in bfloat16 or wider, within the bound.
A program may use at most 64 MiB of HBM per device.

v0:
```python
import jax
import jax.numpy as jnp
from jax import lax
from jax.sharding import PartitionSpec as P

PATCHES = 256


EPS = 1e-06


def on_device(tokens, grad_out, gain, qkv_weight, out_weight):
    tok_rows, local_width = tokens.shape
    model_width = local_width * lax.axis_size("sec")
    head_size = out_weight.shape[0]
    images = tok_rows // PATCHES
    tok_float = tokens.astype(jnp.float32)
    row_sums, row_squares = lax.psum(
        (jnp.sum(tok_float, axis=1), jnp.sum(tok_float * tok_float, axis=1)), "sec"
    )
    row_mean = row_sums / model_width
    row_var = row_squares / model_width - row_mean * row_mean
    inv_std = lax.rsqrt(row_var + EPS)
    normed = (tok_float - row_mean[:, None]) * inv_std[:, None]
    hidden = (normed * gain[None, :]).astype(jnp.bfloat16)
    columns = hidden
    partial_value = jnp.dot(
        columns,
        lax.all_gather(qkv_weight, "fsdp", axis=0, tiled=True),
        preferred_element_type=jnp.float32,
    )
    proj = lax.psum(partial_value, "sec").astype(jnp.bfloat16)
    parts = proj.reshape(images, PATCHES, 3, head_size)
    query, key_in, value = (parts[:, :, 0], parts[:, :, 1], parts[:, :, 2])
    scale = 1.0 / head_size**0.5
    scores = jnp.einsum("ipd,iqd->ipq", query, key_in, preferred_element_type=jnp.float32) * scale
    probs = jax.nn.softmax(scores, axis=-1)
    probs_b = probs.astype(jnp.bfloat16)
    attended = jnp.einsum(
        "ipq,iqd->ipd", probs_b, value, preferred_element_type=jnp.float32
    ).astype(jnp.bfloat16)
    attended = attended.reshape(tok_rows, head_size)
    local_outw = lax.dot_general(
        attended, grad_out, (((0,), (0,)), ((), ())), preferred_element_type=jnp.float32
    )
    grad_outw = lax.psum_scatter(local_outw, "fsdp", scatter_dimension=1, tiled=True)
    columns = grad_out
    att_partial = lax.dot_general(
        columns,
        lax.all_gather(out_weight, "fsdp", axis=1, tiled=True),
        (((1,), (1,)), ((), ())),
        preferred_element_type=jnp.float32,
    )
    grad_att = lax.psum(att_partial, "sec").astype(jnp.bfloat16)
    grad_att3 = grad_att.reshape(images, PATCHES, head_size)
    grad_prob = jnp.einsum("ipd,iqd->ipq", grad_att3, value, preferred_element_type=jnp.float32)
    grad_score = (
        probs * (grad_prob - jnp.sum(grad_prob * probs, axis=-1, keepdims=True)) * scale
    ).astype(jnp.bfloat16)
    grad_query = jnp.einsum("ipq,iqd->ipd", grad_score, key_in, preferred_element_type=jnp.float32)
    grad_key = jnp.einsum("ipq,ipd->iqd", grad_score, query, preferred_element_type=jnp.float32)
    grad_value = jnp.einsum("ipq,ipd->iqd", probs_b, grad_att3, preferred_element_type=jnp.float32)
    grad_proj = (
        jnp.stack([grad_query, grad_key, grad_value], axis=2)
        .reshape(tok_rows, 3 * head_size)
        .astype(jnp.bfloat16)
    )
    local_qkv = lax.dot_general(
        hidden, grad_proj, (((0,), (0,)), ((), ())), preferred_element_type=jnp.float32
    )
    grad_hidden = lax.dot_general(
        grad_proj,
        lax.all_gather(qkv_weight, "fsdp", axis=0, tiled=True),
        (((1,), (1,)), ((), ())),
        preferred_element_type=jnp.float32,
    )
    local_gain = jnp.sum(grad_hidden * normed, axis=0)
    grad_normed = grad_hidden * gain[None, :]
    first_sum, second_sum = lax.psum(
        (jnp.sum(grad_normed, axis=1), jnp.sum(grad_normed * normed, axis=1)), "sec"
    )
    first = first_sum / model_width
    second = second_sum / model_width
    grad_tokens = grad_out.astype(jnp.float32) + inv_std[:, None] * (
        grad_normed - first[:, None] - normed * second[:, None]
    )
    grad_qkv, grad_gain = (
        lax.psum_scatter(local_qkv, "fsdp", scatter_dimension=0, tiled=True),
        lax.psum_scatter(local_gain, "fsdp", scatter_dimension=0, tiled=True),
    )
    return (grad_tokens.astype(jnp.bfloat16), grad_qkv, grad_outw, grad_gain)


def solution(mesh):
    placed = (
        P("fsdp", "sec"),
        P("fsdp", "sec"),
        P("sec"),
        P(("sec", "fsdp"), None),
        P(None, ("sec", "fsdp")),
    )
    return jax.shard_map(
        on_device,
        mesh=mesh,
        in_specs=placed,
        out_specs=(
            P("fsdp", "sec"),
            P(("sec", "fsdp"), None),
            P(None, ("sec", "fsdp")),
            P(("sec", "fsdp")),
        ),
        check_vma=False,
    )
```

profile of v0, /device:TPU:0, one launch (start us, length us, event | category | flops | bytes accessed | tf_op | source)
XLA Modules:
  0.0 233.5 jit_solution(10259902280410637846)
XLA Ops:
  7.2 0.0 copy-start.1
  7.2 0.0 copy-start.4
  7.2 0.0 all-gather.2.cloned.1.call-start
  7.2 0.7 all-gather.2.cloned.1.call-update
  7.9 0.0 reduce-scatter.5.cloned.1.call-start
  8.0 33.2 %all_gather.8 = bf16[128,1536]{0,1:T(8,128)(2,1)S(1)} all-gather(bf16[128,192]{0,1:T(8,128)(2,1)} %param.9), channel_id=1, replica_groups=mesh['sec'=4,'fsdp'=8] {'fsdp'}, dimensions={1}, use_global_device_ids=true | all-gather | bytes 442368 | tf_op jit(solution)/shard_map/all_gather | solution.py:50
  41.2 2.0 fusion.45
  43.2 0.0 copy-done.1
  43.2 0.5 fusion.2
  43.7 6.1 %all-reduce.3 = (f32[512]{0:T(512)S(1)}, f32[512]{0:T(512)S(1)}) all-reduce(f32[512]{0:T(512)S(1)} %get-tuple-element.8, f32[512]{0:T(512)S(1)} %get-tuple-element.7), channel_id=1, replica_groups=mesh['sec'=4,'fsdp'=8] {'sec'}, use_global_device_ids=true, to_apply=%region_3.0 | all-reduce | flops 1024 | bytes 8192 | tf_op jit(solution)/shard_map/psum | solution.py:18
  49.8 0.0 copy-start.5
  49.8 0.0 copy-start.6
  49.8 4.9 %all-gather.2.cloned.1.call-done = bf16[1536,384]{1,0:T(8,128)(2,1)} async-done(((bf16[192,384]{1,0:T(8,128)(2,1)}), bf16[1536,384]{1,0:T(8,128)(2,1)}) %all-gather.2.cloned.1.call-update) | async-done | bytes 1179664 | tf_op jit(solution)/shard_map/all_gather | solution.py:29
  54.7 0.0 copy-done.4
  54.7 2.3 fusion.41
  57.0 25.2 %all-reduce.5 = (bf16[512,128]{1,0:T(8,128)(2,1)}, bf16[512,384]{1,0:T(8,128)(2,1)S(1)}) all-reduce(f32[512,128]{1,0:T(8,128)S(1)} %fusion.45, f32[512,384]{1,0:T(8,128)S(1)} %fusion.41), channel_id=1, replica_groups=mesh['sec'=4,'fsdp'=8] {'sec'}, use_global_device_ids=true, to_apply=%region_7.0 | all-reduce | flops 262144 | bytes 1572864 | tf_op jit(solution)/shard_map/psum | solution.py:54
  82.2 0.0 copy-start
  82.2 0.9 reshape.31
  83.2 3.1 %fusion.43 = (bf16[2,256,1,128]{3,2,1,0:T(2,128)(2,1)S(1)}, bf16[2,256,1,128]{3,2,1,0:T(2,128)(2,1)}, bf16[2,256,1,128]{3,2,1,0:T(2,128)(2,1)}) fusion(bf16[2,256,3,128]{3,2,1,0:T(4,128)(2,1)} %reshape.31), kind=kLoop, calls=%fused_computation.58 | loop fusion | bytes 786432 | tf_op jit(solution)/shard_map/slice | solution.py:34
  86.3 2.7 %fusion.44 = (f32[2,256]{1,0:T(2,128)}, f32[2,256,256]{1,2,0:T(8,128)}) fusion(bf16[2,256,1,128]{3,2,1,0:T(2,128)(2,1)} %get-tuple-element.17, bf16[2,256,1,128]{3,2,1,0:T(2,128)(2,1)} %get-tuple-element.16), kind=kOutput, calls=%fused_computation.59 | convolution fusion | flops 33947904 | bytes 788480 | tf_op jit(solution)/shard_map/sub | solution.py:37
  89.0 1.6 convolution_convert_fusion
  90.6 0.0 copy-done
  90.6 1.6 fusion.46
  92.2 0.0 copy-start.3
  92.2 0.0 reduce-scatter.5.cloned.1.call-update
  92.3 0.0 reduce-scatter.3.cloned.1.call-start
  92.3 1.9 fusion.32
  94.2 0.0 copy-start.2
  94.2 2.7 %fusion.21 = bf16[2,256,1,128]{3,1,0,2:T(8,128)(2,1)} fusion(f32[2,256,256]{1,2,0:T(8,128)} %fusion.32, bf16[2,256,1,128]{3,2,1,0:T(2,128)(2,1)} %get-tuple-element.16, f32[2,256,256]{1,2,0:T(8,128)} %get-tuple-element.21, f32[2,256]{1,0:T(2,128)} %get-tuple-element.20), kind=kOutput, calls=%fused_computation.30 | convolution fusion | flops 34538240 | bytes 1312768 | tf_op jit(solution)/shard_map/ipq,iqd->ipd/dot_general | solution.py:60
  96.9 0.0 copy-done.3
  96.9 2.2 fusion.23
  99.1 0.0 copy-done.2
  99.1 2.5 %fusion.22 = bf16[2,256,1,128]{3,1,0,2:T(8,128)(2,1)} fusion(f32[2,256,256]{1,2,0:T(8,128)} %fusion.32, bf16[2,256,1,128]{3,2,1,0:T(2,128)(2,1)S(1)} %copy-done.2, f32[2,256,256]{1,2,0:T(8,128)} %get-tuple-element.21, f32[2,256]{1,0:T(2,128)} %get-tuple-element.20), kind=kOutput, calls=%fused_computation.31 | convolution fusion | flops 34538240 | bytes 1312768 | tf_op jit(solution)/shard_map/ipq,ipd->iqd/dot_general | solution.py:61
  101.7 1.1 pad_maximum_fusion
  102.7 1.1 copy.26
  103.8 1.1 copy.35
  104.9 0.0 copy-done.5
  104.9 0.0 copy-done.6
  104.9 2.7 %fusion.39 = f32[1536,384]{1,0:T(8,128)} fusion(bf16[512,384]{0,1:T(8,128)(2,1)S(1)} %bitcast.65, bf16[512,1536]{1,0:T(8,128)(2,1)S(1)} %copy-done.1, f32[1536]{0:T(1024)S(1)} %copy-done.4, f32[512]{0:T(512)S(1)} %get-tuple-element.19, f32[512]{0:T(512)S(1)} %get-tuple-element.18), kind=kOutput, calls=%fused_computation.56 | convolution fusion | flops 607911936 | bytes 4335616 | tf_op jit(solution)/shard_map/dot_general | solution.py:68
  107.6 0.0 reduce-scatter.3.cloned.1.call-update
  107.6 1.2 dynamic-slice
  109.5 5.2 %fusion.14 = (f32[1536]{0:T(1024)S(1)}, f32[512]{0:T(512)}, f32[512]{0:T(512)}, f32[512,1536]{1,0:T(8,128)}) fusion(bf16[512,1536]{1,0:T(8,128)(2,1)S(1)} %copy-done.1, f32[512]{0:T(512)} %copy-done.6, f32[512]{0:T(512)} %copy-done.5, f32[1536]{0:T(1024)S(1)} %copy-done.4, bf16[512,384]{0,1:T(8,128)(2,1)S(1)} %bitcast.66, ...), kind=kOutput, calls=%fused_computation.17 | convolution fusion | flops 611055104 | bytes 6311936 | tf_op jit(solution)/shard_map/dot_general | solution.py:71
  114.7 19.6 %all-reduce = f32[1536]{0:T(1024)S(1)} all-reduce(f32[1536]{0:T(1024)S(1)} %get-tuple-element.4), channel_id=4, replica_groups=mesh['sec'=4,'fsdp'=8] {'fsdp'}, use_global_device_ids=true, to_apply=%region_16.0.clone | all-reduce | flops 1536 | bytes 12288
  134.4 0.6 dynamic-slice.1
  135.0 5.8 %all-reduce.1 = (f32[512]{0:T(512)S(1)}, f32[512]{0:T(512)S(1)}) all-reduce(f32[512]{0:T(512)} %get-tuple-element.5, f32[512]{0:T(512)} %get-tuple-element.6), channel_id=1, replica_groups=mesh['sec'=4,'fsdp'=8] {'sec'}, use_global_device_ids=true, to_apply=%region_12.0 | all-reduce | flops 1024 | bytes 8192 | tf_op jit(solution)/shard_map/psum | solution.py:79
  140.8 4.4 %fusion.13 = bf16[512,1536]{1,0:T(8,128)(2,1)} fusion(bf16[512,1536]{1,0:T(8,128)(2,1)S(1)} %copy-done.1, bf16[512,1536]{1,0:T(8,128)(2,1)S(1)} %copy-done, f32[512,1536]{1,0:T(8,128)} %get-tuple-element.22, f32[512]{0:T(512)S(1)} %get-tuple-element.23, f32[512]{0:T(512)S(1)} %get-tuple-element.24, f32[1536]{0:T(1024)S(1)} %copy-done.4, f32[512]{0:T(512)} %copy-done.6, ...), kind=kLoop, calls=%fused_computation.16 | loop fusion | flops 8650752 | bytes 7878656 | tf_op jit(solution)/shard_map/convert_element_type | solution.py:91
  145.1 9.4 %reduce-scatter.5.cloned.1.call-done = f32[128,192]{0,1:T(8,128)} async-done(((f32[128,1536]{0,1:T(8,128)}), f32[128,192]{0,1:T(8,128)}) %reduce-scatter.5.cloned.1.call-update) | async-done | bytes 98320 | tf_op jit(solution)/shard_map/reduce_scatter | solution.py:46
  154.5 72.4 %reduce-scatter.3.cloned.1.call-done = f32[192,384]{1,0:T(8,128)} async-done(((f32[1536,384]{1,0:T(8,128)}), f32[192,384]{1,0:T(8,128)}) %reduce-scatter.3.cloned.1.call-update) | async-done | bytes 294928 | tf_op jit(solution)/shard_map/reduce_scatter | solution.py:88
  (2 shorter events, 0.0 us)
Async XLA Ops:
  7.2 36.0 %copy-start.1 = (bf16[512,1536]{1,0:T(8,128)(2,1)S(1)}, bf16[512,1536]{1,0:T(8,128)(2,1)}, u32[]{:S(2)}) copy-start(bf16[512,1536]{1,0:T(8,128)(2,1)} %param.5) | copy-start | bytes 4718596
  7.2 47.5 %copy-start.4 = (f32[1536]{0:T(1024)S(1)}, f32[1536]{0:T(1024)}, u32[]{:S(2)}) copy-start(f32[1536]{0:T(1024)} %param.7) | copy-start | bytes 18436
  7.2 47.5 %all-gather.2.cloned.1.call-start = ((), (), s32[]{:S(2)}) async-start(), calls=%async_computation.2 | async-start | bytes 1327104 | tf_op jit(solution)/shard_map/all_gather | solution.py:29
  7.9 146.6 %reduce-scatter.5.cloned.1.call-start = ((), (), s32[]{:S(2)}) async-start(), calls=%async_computation.4 | async-start | bytes 884736 | tf_op jit(solution)/shard_map/reduce_scatter | solution.py:46
  49.8 55.1 %copy-start.5 = (f32[512]{0:T(512)}, f32[512]{0:T(512)S(1)}, u32[]{:S(2)}) copy-start(f32[512]{0:T(512)S(1)} %get-tuple-element.18) | copy-start | bytes 6148
  49.8 55.1 %copy-start.6 = (f32[512]{0:T(512)}, f32[512]{0:T(512)S(1)}, u32[]{:S(2)}) copy-start(f32[512]{0:T(512)S(1)} %get-tuple-element.19) | copy-start | bytes 6148
  82.2 8.4 %copy-start = (bf16[512,1536]{1,0:T(8,128)(2,1)S(1)}, bf16[512,1536]{1,0:T(8,128)(2,1)}, u32[]{:S(2)}) copy-start(bf16[512,1536]{1,0:T(8,128)(2,1)} %param.6) | copy-start | bytes 4718596
  92.2 4.7 %copy-start.3 = (bf16[512,128]{1,0:T(8,128)(2,1)S(1)}, bf16[512,128]{1,0:T(8,128)(2,1)}, u32[]{:S(2)}) copy-start(bf16[512,128]{1,0:T(8,128)(2,1)} %get-tuple-element.11) | copy-start | bytes 393220
  92.3 134.7 %reduce-scatter.3.cloned.1.call-start = ((), (), s32[]{:S(2)}) async-start(), calls=%async_computation.3 | async-start | bytes 2654208 | tf_op jit(solution)/shard_map/reduce_scatter | solution.py:88
  94.2 4.9 %copy-start.2 = (bf16[2,256,1,128]{3,2,1,0:T(2,128)(2,1)S(1)}, bf16[2,256,1,128]{3,2,1,0:T(2,128)(2,1)}, u32[]{:S(2)}) copy-start(bf16[2,256,1,128]{3,2,1,0:T(2,128)(2,1)} %get-tuple-element.17) | copy-start | bytes 393220
Sparse Core Ops, SparseCore 0:
  10.2 44.4 all-gather.1
  92.4 62.0 reduce-scatter.4
  159.0 67.9 reduce-scatter.2
where the time goes:
time: 234 us
  blocking collectives  89.9 us (38%)
  waiting for transfers between devices  87.5 us (37%)
  matrix products  27.5 us (12%)
  between operations  14.5 us (6%)
  local copies, waits for them, and re-layouts  8.06 us (3%)
  other arithmetic  5.98 us (3%)
    reduce_scatter x1, waiting for transfers between devices, on_device(): lax.psum_scatter(local_qkv, 'fsdp', scatter_dimension=0, tiled=True)  72.4 us
    all_gather x1, blocking collectives, on_device(): lax.all_gather(out_weight, 'fsdp', axis=1, tiled=True)  33.2 us
    psum x1, blocking collectives, on_device(): grad_att = lax.psum(att_partial, 'sec').astype(jnp.bfloat16)  25.2 us
    unnamed x1, blocking collectives  19.6 us
    reduce_scatter x1, waiting for transfers between devices, on_device(): lax.psum_scatter(local_outw, 'fsdp', scatter_dimension=1, tiled=True)  9.4 us
    psum x1, blocking collectives, on_device(): lax.psum((jnp.sum(tok_float, axis=1), jnp.sum(tok_float * tok_float, axis...  6.06 us
    psum x1, blocking collectives, on_device(): lax.psum((jnp.sum(grad_normed, axis=1), jnp.sum(grad_normed * normed, axi...  5.76 us
    dot_general x1, matrix products, on_device(): lax.dot_general(grad_proj, lax.all_gather(qkv_weight, 'fsdp', axis=0, til...  5.22 us
  transfers between devices with their start and end apart: 3, of which 3 were waited for; matrix products, arithmetic and copies ran while one was open for 13% of the time, Pallas kernels for 0%

commit v1 on v0

--- a/solution.py
+++ b/solution.py
@@ -1,15 +1,579 @@
+import functools
+
 import jax
 import jax.numpy as jnp
 from jax import lax
+from jax.experimental import pallas as pl
+from jax.experimental.pallas import tpu as pltpu
 from jax.sharding import PartitionSpec as P
 
 PATCHES = 256
-
-
 EPS = 1e-06
+MESH = pl.DeviceIdType.MESH
+F32 = jnp.float32
+BF16 = jnp.bfloat16
+
+
+def nn(a, b):
+    return jnp.dot(a, b, preferred_element_type=F32)
+
+
+def nt(a, b):
+    return lax.dot_general(a, b, (((1,), (1,)), ((), ())), preferred_element_type=F32)
+
+
+def tn(a, b):
+    return lax.dot_general(a, b, (((0,), (0,)), ((), ())), preferred_element_type=F32)
+
+
+def copy_to(src, dst, send, recv, device):
+    return pltpu.make_async_remote_copy(
+        src_ref=src,
+        dst_ref=dst,
+        send_sem=send,
+        recv_sem=recv,
+        device_id=device,
+        device_id_type=MESH,
+    )
+
+
+def kernel(
+    nz,
+    width,
+    tok_ref,
+    go_ref,
+    gain_ref,
+    qkv_ref,
+    ow_ref,
+    gt_ref,
+    grad_ref,
+    weights,
+    hidden,
+    hidden_t,
+    go_t,
+    stats,
+    mean_inv,
+    first_out,
+    first_own,
+    first_in,
+    second_out,
+    second_in,
+    gp,
+    moments,
+    sums,
+    y_out,
+    y_in,
+    own,
+    left_out,
+    right_out,
+    left_in,
+    right_in,
+    gather_send,
+    gather_recv,
+    stat_send,
+    stat_recv,
+    core_send,
+    core_recv,
+    x_send,
+    x_recv,
+    gp_send,
+    gp_recv,
+    y_send,
+    y_recv,
+    chain_send,
+    chain_recv,
+):
+    rows, local = tok_ref.shape
+    depth, head = ow_ref.shape
+    groups = weights.shape[0]
+    half = rows // 2
+    s = lax.axis_index("sec")
+    f = lax.axis_index("fsdp")
+    z, y = f // 2, f % 2
+    c = s % 2
+    core = {"sec": s + 1 - 2 * c}
+    across = {"sec": (s + 2) % 4}
+    other_y = {"fsdp": f + 1 - 2 * y}
+    to_left = {"fsdp": f - 2}
+    to_right = {"fsdp": f + 2}
+    has_left = z > 0
+    has_right = z < nz - 1
+
+    barrier = pltpu.get_barrier_semaphore()
+
+    def greet(device):
+        pl.semaphore_signal(barrier, inc=1, device_id=device, device_id_type=MESH)
+
+    greet(other_y)
+    for k in range(1, 4):
+        greet({"sec": (s + k) % 4})
+    pl.when(has_left)(lambda: greet(to_left))
+    pl.when(has_right)(lambda: greet(to_right))
+
+    mine = pl.ds(pl.multiple_of(f * depth, depth), depth)
+    weights[0, mine, :] = ow_ref[...]
+    for g in range(1, groups):
+        weights[g, mine, :] = qkv_ref[:, (g - 1) * head : g * head]
+
+    peers = 4 + has_left.astype(jnp.int32) + has_right.astype(jnp.int32)
+    pl.semaphore_wait(barrier, peers)
+
+    def block(g, shard):
+        return weights.at[g, pl.ds(pl.multiple_of(shard * depth, depth), depth), :]
+
+    def gather_copy(g, shard_z, way, device):
+        shard = shard_z * 2 + y
+        ref = block(g, shard)
+        return copy_to(
+            ref, ref, gather_send.at[g, way, shard_z], gather_recv.at[g, shard], device
+        )
+
+    def go_left(g, shard_z):
+        return gather_copy(g, shard_z, 0, to_left)
+
+    def go_right(g, shard_z):
+        return gather_copy(g, shard_z, 1, to_right)
+
+    def go_y(g, shard_z):
+        return gather_copy(g, shard_z, 2, other_y)
+
+    def arrived(g, shard):
+        ref = block(g, shard)
+        copy_to(
+            ref, ref, gather_send.at[g, 0, 0], gather_recv.at[g, shard], other_y
+        ).wait_recv()
+
+    def send_own(g):
+        pl.when(has_left)(lambda: go_left(g, z).start())
+        pl.when(has_right)(lambda: go_right(g, z).start())
+        go_y(g, z).start()
+
+    def forward(g):
+        for d in range(1, nz):
+
+            @pl.when(z - d >= 0)
+            def _():
+                arrived(g, (z - d) * 2 + y)
+                pl.when(has_right)(lambda: go_right(g, z - d).start())
+                go_y(g, z - d).start()
+
+            @pl.when(z + d < nz)
+            def _():
+                arrived(g, (z + d) * 2 + y)
+                pl.when(has_left)(lambda: go_left(g, z + d).start())
+                go_y(g, z + d).start()
+
+    def gathered(g):
+        for shard_z in range(nz):
+            arrived(g, shard_z * 2 + 1 - y)
+
+    def gather_sent():
+        for g in range(groups):
+            for shard_z in range(nz):
+                pl.when(has_left & (z <= shard_z))(lambda: go_left(g, shard_z).wait_send())
+                pl.when(has_right & (z >= shard_z))(lambda: go_right(g, shard_z).wait_send())
+                go_y(g, shard_z).wait_send()
+
+    send_own(0)
+    send_own(1)
+
+    step = 64
+    lane = lax.broadcasted_iota(jnp.int32, (step, 128), 1)
+
+    def row_sums(i, carry):
+        r = pl.ds(pl.multiple_of(i * step, step), step)
+        t = tok_ref[r, :].astype(F32)
+        a = jnp.sum(t, axis=1, keepdims=True)
+        b = jnp.sum(t * t, axis=1, keepdims=True)
+        mean_inv[r, :] = jnp.where(lane == 0, a, b)
+        return carry
+
+    lax.fori_loop(0, rows // step, row_sums, 0)
+    stats[s] = mean_inv[...].T[:8, :]
+
+    def stat_copy(k):
+        return copy_to(
+            stats.at[s], stats.at[s], stat_send.at[k], stat_recv.at[s], {"sec": (s + k) % 4}
+        )
+
+    for k in range(1, 4):
+        stat_copy(k).start()
+
+    forward(0)
+    send_own(2)
+
+    tstep = 256
+
+    def turn(src, dst):
+        for i in range(rows // tstep):
+
+            def body(j, carry):
+                cols = pl.ds(pl.multiple_of(j * tstep, tstep), tstep)
+                part = src[i * tstep : (i + 1) * tstep, cols].astype(F32)
+                dst[cols, i * tstep : (i + 1) * tstep] = part.T.astype(BF16)
+                return carry
+
+            lax.fori_loop(0, local // tstep, body, 0)
+
+    turn(go_ref, go_t)
+
+    gain_row = gain_ref[...]
+    g_hi = gain_row.astype(BF16)
+    rest = gain_row - g_hi.astype(F32)
+    g_mid = rest.astype(BF16)
+    g_lo = (rest - g_mid.astype(F32)).astype(BF16)
+    row16 = lax.broadcasted_iota(jnp.int32, (16, local), 0)
+    gain16 = jnp.where(
+        row16 == 0,
+        g_hi.astype(F32),
+        jnp.where(row16 == 1, g_mid.astype(F32), jnp.where(row16 == 2, g_lo.astype(F32), 0.0)),
+    ).astype(BF16)
+
+    my_rows = pl.ds(pl.multiple_of(c * half, half), half)
+    their_rows = pl.ds(pl.multiple_of((1 - c) * half, half), half)
+
+    def core_copy(g):
+        return copy_to(
+            first_out.at[g], first_in.at[g], core_send.at[g], core_recv.at[g], core
+        )
+
+    def x_copy(g):
+        return copy_to(
+            second_out.at[g], second_in.at[g], x_send.at[g], x_recv.at[g], across
+        )
+
+    def project(g, left):
+        w = weights[g]
+        u = jnp.sum(nn(gain16, w), axis=0, keepdims=True)
+        u = jnp.broadcast_to(u, (8, head))
+        first_out[g, half : half + 8, :] = u
+        first_out[g, 0:half, :] = nn(left[their_rows, :], w)
+        core_copy(g).start()
+        first_own[g, half : half + 8, :] = u
+        first_own[g, 0:half, :] = nn(left[my_rows, :], w)
+
+    def across_start(g):
+        core_copy(g).wait_recv()
+        second_out[g] = first_own[g] + first_in[g]
+        x_copy(g).start()
+
+    gathered(0)
+    project(0, go_ref)
+    forward(1)
+    send_own(3)
+
+    for k in range(1, 4):
+        sender = (s + k) % 4
+        copy_to(
+            stats.at[sender], stats.at[sender], stat_send.at[k], stat_recv.at[sender], core
+        ).wait_recv()
+    total = stats[0] + stats[1] + stats[2] + stats[3]
+    row_mean = total[0:1, :] / width
+    row_var = total[1:2, :] / width - row_mean * row_mean
+    inv_std = lax.rsqrt(row_var + EPS)
+    sub = lax.broadcasted_iota(jnp.int32, (128, rows), 0)
+    mean_inv[...] = jnp.where(sub == 0, row_mean, inv_std).T
+
+    def norm(i, carry):
+        r = pl.ds(pl.multiple_of(i * step, step), step)
+        t = tok_ref[r, :].astype(F32)
+        m = mean_inv[r, :]
+        normed = (t - m[:, 0:1]) * m[:, 1:2]
+        hidden[r, :] = (normed * gain_ref[...]).astype(BF16)
+        return carry
+
+    lax.fori_loop(0, rows // step, norm, 0)
+
+    across_start(0)
+    gathered(1)
+    project(1, hidden)
+    forward(2)
+    across_start(1)
+    gathered(2)
+    project(2, hidden)
+    forward(3)
+    across_start(2)
+    turn(hidden, hidden_t)
+    gathered(3)
+    project(3, hidden)
+    across_start(3)
+
+    def finish(g):
+        x_copy(g).wait_recv()
+        sums[g] = second_out[g] + second_in[g]
+
+    for g in range(groups):
+        finish(g)
+
+    scale = 1.0 / head**0.5
+    grad_att = sums[0, 0:half, :].astype(BF16)
+    query = sums[1, 0:half, :].astype(BF16)
+    key = sums[2, 0:half, :].astype(BF16)
+    value = sums[3, 0:half, :].astype(BF16)
+    scores = nt(query, key) * scale
+    e = jnp.exp(scores - jnp.max(scores, axis=-1, keepdims=True))
+    probs = e / jnp.sum(e, axis=-1, keepdims=True)
+    probs_b = probs.astype(BF16)
+    gp[my_rows, 0:head] = nn(probs_b, value).astype(BF16)
+
+    def gp_copy(k):
+        ref = (
+            gp.at[my_rows, pl.ds(0, head)],
+            gp.at[my_rows, pl.ds(head, 3 * head)],
+            moments.at[my_rows, :],
+        )[k]
+        return copy_to(ref, ref, gp_send.at[k], gp_recv.at[k], core)
+
+    def gp_arrived(k):
+        ref = (
+            gp.at[their_rows, pl.ds(0, head)],
+            gp.at[their_rows, pl.ds(head, 3 * head)],
+            moments.at[their_rows, :],
+        )[k]
+        copy_to(ref, ref, gp_send.at[k], gp_recv.at[k], core).wait_recv()
+
+    gp_copy(0).start()
+    grad_prob = nt(grad_att, value)
+    grad_score = (
+        probs * (grad_prob - jnp.sum(grad_prob * probs, axis=-1, keepdims=True)) * scale
+    ).astype(BF16)
+
+    spans = (slice(0, head), slice(head, 4 * head))
+    turned = (go_t, hidden_t)
+    order = []
+    for k in range(nz):
+        order.append(nz - 1 - k // 2 if k % 2 == 0 else k // 2)
+
+    def part(p, shard):
+        r = pl.ds(pl.multiple_of(shard * depth, depth), depth)
+        return nn(turned[p][r, :], gp[:, spans[p]])
+
+    def y_copy(p, shard_z):
+        cols = pl.ds(spans[p].start, spans[p].stop - spans[p].start)
+        return copy_to(
+            y_out.at[shard_z, :, cols],
+            y_in.at[shard_z, :, cols],
+            y_send.at[p, shard_z],
+            y_recv.at[p, shard_z],
+            other_y,
+        )
+
+    def y_phase(p):
+        for shard_z in order:
+            y_out[shard_z, :, spans[p]] = part(p, shard_z * 2 + 1 - y).astype(BF16)
+            y_copy(p, shard_z).start()
+
+    def own_phase(p):
+        for shard_z in order:
+            own[shard_z, :, spans[p]] = part(p, shard_z * 2 + y)
+
+    gp_arrived(0)
+    y_phase(0)
+
+    grad_query = nn(grad_score, key)
+    grad_key = tn(grad_score, query)
+    grad_value = tn(probs_b, grad_att)
+    lane_h = lax.broadcasted_iota(jnp.int32, (half, 128), 1)
+    first = jnp.zeros((half, 1), F32)
+    second = jnp.zeros((half, 1), F32)
+    for g, grad in enumerate((grad_query, grad_key, grad_value)):
+        rounded = grad.astype(BF16)
+        gp[my_rows, (g + 1) * head : (g + 2) * head] = rounded
+        r32 = rounded.astype(F32)
+        u = sums[g + 1, half : half + 1, :]
+        first += jnp.sum(r32 * u, axis=1, keepdims=True)
+        second += jnp.sum(r32 * sums[g + 1, 0:half, :], axis=1, keepdims=True)
+    moments[my_rows, :] = jnp.where(lane_h == 0, first, second) / width
+    gp_copy(1).start()
+    gp_copy(2).start()
+    own_phase(0)
+    gp_arrived(1)
+    y_phase(1)
+    own_phase(1)
+
+    tile = 256
+    gp_arrived(2)
+
+    def token_tile(j):
+        cols = pl.ds(pl.multiple_of(j * tile, tile), tile)
+        grad_hidden = nt(gp[:, head : 2 * head], weights[1, cols, :])
+        for g in range(2, groups):
+            grad_hidden += nt(gp[:, g * head : (g + 1) * head], weights[g, cols, :])
+        m = mean_inv[...]
+        inv = m[:, 1:2]
+        normed = (tok_ref[:, cols].astype(F32) - m[:, 0:1]) * inv
+        mo = moments[...]
+        grad_normed = grad_hidden * gain_ref[:, cols]
+        gt_ref[:, cols] = (
+            go_ref[:, cols].astype(F32)
+            + inv * (grad_normed - mo[:, 0:1] - normed * mo[:, 1:2])
+        ).astype(BF16)
+
+    def chain_copy(p, way, dest):
+        cols = pl.ds(spans[p].start, spans[p].stop - spans[p].start)
+        out, into, device = ((left_out, left_in, to_left), (right_out, right_in, to_right))[way]
+        return copy_to(
+            out.at[dest, :, cols],
+            into.at[dest, :, cols],
+            chain_send.at[p, way, dest],
+            chain_recv.at[p, way, dest],
+            device,
+        )
+
+    steps = []
+    for k in range(nz - 1):
+        steps += [(1, nz - 1 - k), (0, k)]
+
+    def chain(p, between):
+        span = spans[p]
+        for way, dest in steps:
+            out, into = ((left_out, left_in), (right_out, right_in))[way]
+            passes = (z > dest) if way == 0 else (z < dest)
+            follows = has_right if way == 0 else has_left
+            between()
+
+            @pl.when(passes)
+            def _():
+                y_copy(p, dest).wait_recv()
+                here = own[dest, :, span] + y_in[dest, :, span].astype(F32)
+
+                @pl.when(follows)
+                def _():
+                    chain_copy(p, way, dest).wait_recv()
+                    out[dest, :, span] = (here + into[dest, :, span].astype(F32)).astype(BF16)
+
+                @pl.when(jnp.logical_not(follows))
+                def _():
+                    out[dest, :, span] = here.astype(BF16)
+
+                chain_copy(p, way, dest).start()
+
+    def chain_end(p):
+        span = spans[p]
+        y_copy(p, z).wait_recv()
+        grad_ref[:, span] = own[z, :, span] + y_in[z, :, span].astype(F32)
+
+        @pl.when(has_left)
+        def _():
+            chain_copy(p, 1, z).wait_recv()
+            grad_ref[:, span] += right_in[z, :, span].astype(F32)
+
+        @pl.when(has_right)
+        def _():
+            chain_copy(p, 0, z).wait_recv()
+            grad_ref[:, span] += left_in[z, :, span].astype(F32)
+
+    tiles = iter(range(local // tile))
+
+    def between():
+        j = next(tiles, None)
+        if j is not None:
+            token_tile(j)
+
+    chain(0, lambda: None)
+    chain(1, between)
+    for j in tiles:
+        token_tile(j)
+    chain_end(0)
+    chain_end(1)
+
+    gather_sent()
+    for k in range(1, 4):
+        stat_copy(k).wait_send()
+    for g in range(groups):
+        core_copy(g).wait_send()
+        x_copy(g).wait_send()
+    for k in range(3):
+        gp_copy(k).wait_send()
+    for p in range(2):
+        for shard_z in range(nz):
+            y_copy(p, shard_z).wait_send()
+        for way, dest in steps:
+            passes = (z > dest) if way == 0 else (z < dest)
+            pl.when(passes)(lambda: chain_copy(p, way, dest).wait_send())
+
+
+def fused(nz, width, tokens, grad_out, gain, qkv_weight, out_weight):
+    rows, local = tokens.shape
+    head = out_weight.shape[0]
+    depth = qkv_weight.shape[0]
+    half = rows // 2
+    n = 2 * nz
+    vmem = pl.BlockSpec(memory_space=pltpu.VMEM)
+    dma = pltpu.SemaphoreType.DMA
+    exchange = pltpu.VMEM((4, half + 8, head), F32)
+    pieces = pltpu.VMEM((nz, depth, 4 * head), BF16)
+    return pl.pallas_call(
+        functools.partial(kernel, nz, width),
+        out_shape=(
+            jax.ShapeDtypeStruct((rows, local), BF16),
+            jax.ShapeDtypeStruct((depth, 4 * head), F32),
+        ),
+        in_specs=[vmem] * 5,
+        out_specs=(vmem, vmem),
+        scratch_shapes=[
+            pltpu.VMEM((4, local, head), BF16),
+            pltpu.VMEM((rows, local), BF16),
+            pltpu.VMEM((local, rows), BF16),
+            pltpu.VMEM((local, rows), BF16),
+            pltpu.VMEM((4, 8, rows), F32),
+            pltpu.VMEM((rows, 128), F32),
+            exchange,
+            exchange,
+            exchange,
+            exchange,
+            exchange,
+            pltpu.VMEM((rows, 4 * head), BF16),
+            pltpu.VMEM((rows, 128), F32),
+            exchange,
+            pieces,
+            pieces,
+            pltpu.VMEM((nz, depth, 4 * head), F32),
+            pieces,
+            pieces,
+            pieces,
+            pieces,
+            dma((4, 3, nz)),
+            dma((4, n)),
+            dma((4,)),
+            dma((4,)),
+            dma((4,)),
+            dma((4,)),
+            dma((4,)),
+            dma((4,)),
+            dma((3,)),
+            dma((3,)),
+            dma((2, nz)),
+            dma((2, nz)),
+            dma((2, 2, nz)),
+            dma((2, 2, nz)),
+        ],
+        compiler_params=pltpu.CompilerParams(
+            collective_id=0, has_side_effects=True, vmem_limit_bytes=48 * 1024 * 1024
+        ),
+        name="head_backward",
+    )(tokens, grad_out, gain.reshape(1, local), qkv_weight, out_weight.T)
 
 
 def on_device(tokens, grad_out, gain, qkv_weight, out_weight):
+    tok_rows, local_width = tokens.shape
+    model_width = local_width * lax.axis_size("sec")
+    head_size = out_weight.shape[0]
+    shards = lax.axis_size("fsdp")
+    depth = qkv_weight.shape[0]
+    if depth % 64 or tok_rows != 2 * PATCHES or lax.axis_size("sec") != 4 or shards % 2:
+        return by_collectives(tokens, grad_out, gain, qkv_weight, out_weight)
+    grad_tokens, grads = fused(
+        shards // 2, model_width, tokens, grad_out, gain, qkv_weight, out_weight
+    )
+    grad_qkv = grads[:, head_size:]
+    grad_outw = grads[:, :head_size].T
+    own_gain = lax.dynamic_slice_in_dim(gain, lax.axis_index("fsdp") * depth, depth)
+    grad_gain = jnp.sum(qkv_weight.astype(F32) * grad_qkv, axis=1) / own_gain
+    return grad_tokens, grad_qkv, grad_outw, grad_gain
+
+
+def by_collectives(tokens, grad_out, gain, qkv_weight, out_weight):
     tok_rows, local_width = tokens.shape
     model_width = local_width * lax.axis_size("sec")
     head_size = out_weight.shape[0]

time: 234 us -> 85.3 us (0.36)
  blocking collectives: 89.9 us -> 0 us
  waiting for transfers between devices: 87.5 us -> 0 us
  Pallas kernels: 0 us -> 74.9 us
  matrix products: 27.5 us -> 0 us
  between operations: 14.5 us -> 0.64 us
  other arithmetic: 5.98 us -> 2.08 us
    reduce_scatter x2 -> x0, waiting for transfers between devices: 81.8 us -> none  [the longest x1 72.4 us: on_device(): lax.psum_scatter(local_qkv, 'fsdp', scatter_dimension=0, tiled=True)]
    pallas_call x0 -> x1, Pallas kernels: none -> 74.9 us  [fused(): pl.pallas_call(functools.partial(kernel, nz, width), out_shape=(jax.Shape...]
    psum x3 -> x0, blocking collectives: 37 us -> none  [the longest x1 25.2 us: on_device(): grad_att = lax.psum(att_partial, 'sec').astype(jnp.bfloat16)]
    all_gather x1 -> x0, blocking collectives: 33.2 us -> none  [on_device(): lax.all_gather(out_weight, 'fsdp', axis=1, tiled=True)]
    dot_general x10 -> x0, matrix products: 24.8 us -> none  [the longest x1 5.22 us: on_device(): lax.dot_general(grad_proj, lax.all_gather(qkv_weight, 'fsdp', axis=0, til...]
    unnamed x1 -> x0, blocking collectives: 19.6 us -> none
    all_gather x1 -> x0, waiting for transfers between devices: 4.93 us -> none  [on_device(): lax.all_gather(qkv_weight, 'fsdp', axis=0, tiled=True)]
    convert_element_type x1 -> x0, other arithmetic: 4.37 us -> none  [on_device(): return (grad_tokens.astype(jnp.bfloat16), grad_qkv, grad_outw, grad_gain)]
  transfers between devices with their start and end apart: 3 -> 0, of which waited for: 3 -> 0; matrix products, arithmetic and copies ran while one was open for 13% -> 0% of each run, Pallas kernels for 0% -> 0%
where the time goes in v1:
time: 85.3 us; the launch traced here: 84.7 us
  Pallas kernels  74.9 us (88%)
  local copies, waits for them, and re-layouts  7.02 us (8%)
  other arithmetic  2.08 us (2%)
    pallas_call x1, Pallas kernels, fused(): pl.pallas_call(functools.partial(kernel, nz, width), out_shape=(jax.Shape...  74.9 us
    unnamed x9, local copies, waits for them, and re-layouts  5.66 us

profile of v1, /device:TPU:0, one launch (start us, length us, event | category | flops | bytes accessed | tf_op | source)
XLA Modules:
  0.0 84.7 jit_solution(4627537164506904360)
XLA Ops:
  0.6 0.7 reshape.11.gain_ref
  1.3 0.0 copy-start
  1.3 1.4 %copy-done = bf16[512,1536]{1,0:T(8,128)(2,1)S(1)} copy-done((bf16[512,1536]{1,0:T(8,128)(2,1)S(1)}, bf16[512,1536]{1,0:T(8,128)(2,1)}, u32[]{:S(2)}) %copy-start) | copy-done | bytes 1572888
  2.7 0.0 copy-start.1
  2.7 1.4 %copy-done.1 = bf16[512,1536]{1,0:T(8,128)(2,1)S(1)} copy-done((bf16[512,1536]{1,0:T(8,128)(2,1)S(1)}, bf16[512,1536]{1,0:T(8,128)(2,1)}, u32[]{:S(2)}) %copy-start.1) | copy-done | bytes 1572888
  4.2 0.0 copy-start.2
  4.2 0.9 %copy-done.2 = bf16[192,384]{1,0:T(8,128)(2,1)S(1)} copy-done((bf16[192,384]{1,0:T(8,128)(2,1)S(1)}, bf16[192,384]{1,0:T(8,128)(2,1)}, u32[]{:S(2)}) %copy-start.2) | copy-done | bytes 147480
  5.1 0.0 copy-start.3
  5.1 0.8 copy-done.3
  5.9 74.9 %head_backward.1 = (bf16[512,1536]{1,0:T(8,128)(2,1)S(1)}, f32[192,512]{1,0:T(8,128)S(1)}) custom-call(bf16[512,1536]{1,0:T(8,128)(2,1)S(1)} %copy-done, bf16[512,1536]{1,0:T(8,128)(2,1)S(1)} %copy-done.1, f32[1,1536]{1,0:T(1,128)S(1)} %reshape.11.gain_ref, bf16[192,384]{1,0:T(8,128)(2,1)S(1)} %copy-done.2, bf16[192,128]{1,0:T(8,128)(2,1)S(1)} %bitcast.3), custom_call_target="tpu_custom_call" | custom-call | tf_op jit(solution)/shard_map/head_backward/pallas_call | solution.py:506
  80.8 0.7 multiply_reduce_fusion
  81.5 0.7 slice_bitcast_fusion
  82.2 1.3 %dynamic-slice_divide_fusion = f32[192]{0:T(256)} fusion(f32[192]{0:T(256)S(1)} %get-tuple-element.8, f32[1536]{0:T(1024)} %param.7, s32[]{:T(128)S(6)} %select_n.3), kind=kLoop, calls=%fused_computation.2 | loop fusion | flops 192 | bytes 2308 | tf_op jit(solution)/shard_map/div | solution.py:572
  83.5 1.1 %copy.10 = bf16[512,1536]{1,0:T(8,128)(2,1)} copy(bf16[512,1536]{1,0:T(8,128)(2,1)S(1)} %get-tuple-element.14) | data formatting | bytes 3145728
Async XLA Ops:
  1.3 1.4 %copy-start = (bf16[512,1536]{1,0:T(8,128)(2,1)S(1)}, bf16[512,1536]{1,0:T(8,128)(2,1)}, u32[]{:S(2)}) copy-start(bf16[512,1536]{1,0:T(8,128)(2,1)} %tok_ref.1) | copy-start | bytes 4718596
  2.7 1.4 %copy-start.1 = (bf16[512,1536]{1,0:T(8,128)(2,1)S(1)}, bf16[512,1536]{1,0:T(8,128)(2,1)}, u32[]{:S(2)}) copy-start(bf16[512,1536]{1,0:T(8,128)(2,1)} %go_ref.1) | copy-start | bytes 4718596
  4.2 0.9 %copy-start.2 = (bf16[192,384]{1,0:T(8,128)(2,1)S(1)}, bf16[192,384]{1,0:T(8,128)(2,1)}, u32[]{:S(2)}) copy-start(bf16[192,384]{1,0:T(8,128)(2,1)} %qkv_ref.1) | copy-start | bytes 442372
  5.1 0.8 copy-start.3

commit v2 on v1

--- a/solution.py
+++ b/solution.py
@@ -40,17 +40,22 @@
 def kernel(
     nz,
     width,
+    tok_hbm,
+    go_hbm,
+    gain_ref,
+    qkv_hbm,
+    ow_hbm,
+    gt_ref,
+    grad_ref,
+    ggain_ref,
     tok_ref,
     go_ref,
-    gain_ref,
-    qkv_ref,
-    ow_ref,
-    gt_ref,
-    grad_ref,
     weights,
     hidden,
     hidden_t,
     go_t,
+    gain_t,
+    gain_pad,
     stats,
     mean_inv,
     first_out,
@@ -64,10 +69,9 @@
     y_out,
     y_in,
     own,
-    left_out,
-    right_out,
-    left_in,
-    right_in,
+    chain_out,
+    chain_in,
+    load_sem,
     gather_send,
     gather_recv,
     stat_send,
@@ -84,7 +88,7 @@
     chain_recv,
 ):
     rows, local = tok_ref.shape
-    depth, head = ow_ref.shape
+    depth, head = ow_hbm.shape
     groups = weights.shape[0]
     half = rows // 2
     s = lax.axis_index("sec")
@@ -111,9 +115,14 @@
     pl.when(has_right)(lambda: greet(to_right))
 
     mine = pl.ds(pl.multiple_of(f * depth, depth), depth)
-    weights[0, mine, :] = ow_ref[...]
+    loads = [pltpu.make_async_copy(ow_hbm, weights.at[0, mine, :], load_sem.at[0])]
     for g in range(1, groups):
-        weights[g, mine, :] = qkv_ref[:, (g - 1) * head : g * head]
+        part_hbm = qkv_hbm.at[:, pl.ds((g - 1) * head, head)]
+        loads.append(pltpu.make_async_copy(part_hbm, weights.at[g, mine, :], load_sem.at[g]))
+    loads.append(pltpu.make_async_copy(tok_hbm, tok_ref, load_sem.at[4]))
+    loads.append(pltpu.make_async_copy(go_hbm, go_ref, load_sem.at[5]))
+    for load in loads:
+        load.start()
 
     peers = 4 + has_left.astype(jnp.int32) + has_right.astype(jnp.int32)
     pl.semaphore_wait(barrier, peers)
@@ -174,8 +183,11 @@
                 pl.when(has_right & (z >= shard_z))(lambda: go_right(g, shard_z).wait_send())
                 go_y(g, shard_z).wait_send()
 
+    loads[0].wait()
     send_own(0)
+    loads[1].wait()
     send_own(1)
+    loads[4].wait()
 
     step = 64
     lane = lax.broadcasted_iota(jnp.int32, (step, 128), 1)
@@ -200,7 +212,10 @@
         stat_copy(k).start()
 
     forward(0)
+    loads[2].wait()
     send_own(2)
+    loads[3].wait()
+    loads[5].wait()
 
     tstep = 256
 
@@ -216,6 +231,9 @@
             lax.fori_loop(0, local // tstep, body, 0)
 
     turn(go_ref, go_t)
+    forward(1)
+    send_own(3)
+    gain_t[...] = jnp.broadcast_to(gain_ref[...], (128, local)).T
 
     gain_row = gain_ref[...]
     g_hi = gain_row.astype(BF16)
@@ -259,8 +277,6 @@
 
     gathered(0)
     project(0, go_ref)
-    forward(1)
-    send_own(3)
 
     for k in range(1, 4):
         sender = (s + k) % 4
@@ -285,15 +301,15 @@
     lax.fori_loop(0, rows // step, norm, 0)
 
     across_start(0)
+    forward(2)
     gathered(1)
     project(1, hidden)
-    forward(2)
+    forward(3)
     across_start(1)
     gathered(2)
     project(2, hidden)
-    forward(3)
+    turn(hidden, hidden_t)
     across_start(2)
-    turn(hidden, hidden_t)
     gathered(3)
     project(3, hidden)
     across_start(3)
@@ -301,98 +317,143 @@
     def finish(g):
         x_copy(g).wait_recv()
         sums[g] = second_out[g] + second_in[g]
-
-    for g in range(groups):
-        finish(g)
+        return sums[g, 0:half, :].astype(BF16)
 
     scale = 1.0 / head**0.5
-    grad_att = sums[0, 0:half, :].astype(BF16)
-    query = sums[1, 0:half, :].astype(BF16)
-    key = sums[2, 0:half, :].astype(BF16)
-    value = sums[3, 0:half, :].astype(BF16)
+    grad_att = finish(0)
+    query = finish(1)
+    key = finish(2)
     scores = nt(query, key) * scale
     e = jnp.exp(scores - jnp.max(scores, axis=-1, keepdims=True))
     probs = e / jnp.sum(e, axis=-1, keepdims=True)
     probs_b = probs.astype(BF16)
-    gp[my_rows, 0:head] = nn(probs_b, value).astype(BF16)
+
+    def gp_piece(k, r):
+        return moments.at[r, :] if k == groups else gp.at[r, pl.ds(k * head, head)]
 
     def gp_copy(k):
-        ref = (
-            gp.at[my_rows, pl.ds(0, head)],
-            gp.at[my_rows, pl.ds(head, 3 * head)],
-            moments.at[my_rows, :],
-        )[k]
+        ref = gp_piece(k, my_rows)
         return copy_to(ref, ref, gp_send.at[k], gp_recv.at[k], core)
 
     def gp_arrived(k):
-        ref = (
-            gp.at[their_rows, pl.ds(0, head)],
-            gp.at[their_rows, pl.ds(head, 3 * head)],
-            moments.at[their_rows, :],
-        )[k]
+        ref = gp_piece(k, their_rows)
         copy_to(ref, ref, gp_send.at[k], gp_recv.at[k], core).wait_recv()
 
-    gp_copy(0).start()
+    def gp_put(k, result):
+        rounded = result.astype(BF16)
+        gp[my_rows, k * head : (k + 1) * head] = rounded
+        gp_copy(k).start()
+        return rounded
+
+    grad_value = gp_put(3, tn(probs_b, grad_att))
+    value = finish(3)
+    gp_put(0, nn(probs_b, value))
     grad_prob = nt(grad_att, value)
     grad_score = (
         probs * (grad_prob - jnp.sum(grad_prob * probs, axis=-1, keepdims=True)) * scale
     ).astype(BF16)
-
-    spans = (slice(0, head), slice(head, 4 * head))
-    turned = (go_t, hidden_t)
-    order = []
-    for k in range(nz):
-        order.append(nz - 1 - k // 2 if k % 2 == 0 else k // 2)
-
-    def part(p, shard):
-        r = pl.ds(pl.multiple_of(shard * depth, depth), depth)
-        return nn(turned[p][r, :], gp[:, spans[p]])
-
-    def y_copy(p, shard_z):
-        cols = pl.ds(spans[p].start, spans[p].stop - spans[p].start)
-        return copy_to(
-            y_out.at[shard_z, :, cols],
-            y_in.at[shard_z, :, cols],
-            y_send.at[p, shard_z],
-            y_recv.at[p, shard_z],
-            other_y,
-        )
-
-    def y_phase(p):
-        for shard_z in order:
-            y_out[shard_z, :, spans[p]] = part(p, shard_z * 2 + 1 - y).astype(BF16)
-            y_copy(p, shard_z).start()
-
-    def own_phase(p):
-        for shard_z in order:
-            own[shard_z, :, spans[p]] = part(p, shard_z * 2 + y)
-
-    gp_arrived(0)
-    y_phase(0)
-
-    grad_query = nn(grad_score, key)
-    grad_key = tn(grad_score, query)
-    grad_value = tn(probs_b, grad_att)
+    grad_query = gp_put(1, nn(grad_score, key))
+    grad_key = gp_put(2, tn(grad_score, query))
     lane_h = lax.broadcasted_iota(jnp.int32, (half, 128), 1)
     first = jnp.zeros((half, 1), F32)
     second = jnp.zeros((half, 1), F32)
-    for g, grad in enumerate((grad_query, grad_key, grad_value)):
-        rounded = grad.astype(BF16)
-        gp[my_rows, (g + 1) * head : (g + 2) * head] = rounded
-        r32 = rounded.astype(F32)
-        u = sums[g + 1, half : half + 1, :]
+    for g, grad in ((1, grad_query), (2, grad_key), (3, grad_value)):
+        r32 = grad.astype(F32)
+        u = sums[g, half : half + 1, :]
         first += jnp.sum(r32 * u, axis=1, keepdims=True)
-        second += jnp.sum(r32 * sums[g + 1, 0:half, :], axis=1, keepdims=True)
+        second += jnp.sum(r32 * sums[g, 0:half, :], axis=1, keepdims=True)
     moments[my_rows, :] = jnp.where(lane_h == 0, first, second) / width
-    gp_copy(1).start()
-    gp_copy(2).start()
-    own_phase(0)
-    gp_arrived(1)
-    y_phase(1)
-    own_phase(1)
+    gp_copy(groups).start()
+
+    def span(g):
+        return slice(g * head, (g + 1) * head)
+
+    def cols_of(g):
+        return pl.ds(g * head, head)
+
+    near = (z < nz // 2).astype(jnp.int32)
+
+    def far_end(way, k):
+        return way * (nz - 1 - k) + (1 - way) * k
+
+    def part(g, shard):
+        r = pl.ds(pl.multiple_of(shard * depth, depth), depth)
+        return nn((go_t if g == 0 else hidden_t)[r, :], gp[:, span(g)])
+
+    def y_copy(g, shard_z):
+        return copy_to(
+            y_out.at[shard_z, :, cols_of(g)],
+            y_in.at[shard_z, :, cols_of(g)],
+            y_send.at[g, shard_z],
+            y_recv.at[g, shard_z],
+            other_y,
+        )
+
+    def y_phase(g):
+        gp_arrived(g)
+        for k in range(nz):
+            shard_z = far_end(near, k)
+            y_out[shard_z, :, span(g)] = part(g, shard_z * 2 + 1 - y).astype(BF16)
+            y_copy(g, shard_z).start()
+
+    def own_phase(g):
+        for k in range(nz):
+            own[k, :, span(g)] = part(g, k * 2 + y)
+
+    def chain_copy(g, way, dest):
+        return copy_to(
+            chain_out.at[way, dest, :, cols_of(g)],
+            chain_in.at[way, dest, :, cols_of(g)],
+            chain_send.at[g, way, dest],
+            chain_recv.at[g, way, dest],
+            {"fsdp": f + 4 * way - 2},
+        )
+
+    def chain(g):
+        for way in (near, 1 - near):
+            follows = ((way == 1) & has_left) | ((way == 0) & has_right)
+            for k in range(nz - 1):
+                dest = far_end(way, k)
+                passes = ((way == 1) & (dest > z)) | ((way == 0) & (dest < z))
+
+                @pl.when(passes)
+                def _():
+                    y_copy(g, dest).wait_recv()
+                    here = own[dest, :, span(g)] + y_in[dest, :, span(g)].astype(F32)
+
+                    @pl.when(follows)
+                    def _():
+                        chain_copy(g, way, dest).wait_recv()
+                        chain_out[way, dest, :, span(g)] = (
+                            here + chain_in[way, dest, :, span(g)].astype(F32)
+                        ).astype(BF16)
+
+                    @pl.when(jnp.logical_not(follows))
+                    def _():
+                        chain_out[way, dest, :, span(g)] = here.astype(BF16)
+
+                    chain_copy(g, way, dest).start()
+
+    def chain_end(g):
+        y_copy(g, z).wait_recv()
+        grad_ref[:, span(g)] = own[z, :, span(g)] + y_in[z, :, span(g)].astype(F32)
+
+        @pl.when(has_left)
+        def _():
+            chain_copy(g, 1, z).wait_recv()
+            grad_ref[:, span(g)] += chain_in[1, z, :, span(g)].astype(F32)
+
+        @pl.when(has_right)
+        def _():
+            chain_copy(g, 0, z).wait_recv()
+            grad_ref[:, span(g)] += chain_in[0, z, :, span(g)].astype(F32)
+
+        if g == 0:
+            return 0.0
+        held = weights[g, mine, :].astype(F32)
+        return jnp.sum(held * grad_ref[:, span(g)], axis=1, keepdims=True)
 
     tile = 256
-    gp_arrived(2)
 
     def token_tile(j):
         cols = pl.ds(pl.multiple_of(j * tile, tile), tile)
@@ -409,73 +470,29 @@
             + inv * (grad_normed - mo[:, 0:1] - normed * mo[:, 1:2])
         ).astype(BF16)
 
-    def chain_copy(p, way, dest):
-        cols = pl.ds(spans[p].start, spans[p].stop - spans[p].start)
-        out, into, device = ((left_out, left_in, to_left), (right_out, right_in, to_right))[way]
-        return copy_to(
-            out.at[dest, :, cols],
-            into.at[dest, :, cols],
-            chain_send.at[p, way, dest],
-            chain_recv.at[p, way, dest],
-            device,
-        )
-
-    steps = []
-    for k in range(nz - 1):
-        steps += [(1, nz - 1 - k), (0, k)]
-
-    def chain(p, between):
-        span = spans[p]
-        for way, dest in steps:
-            out, into = ((left_out, left_in), (right_out, right_in))[way]
-            passes = (z > dest) if way == 0 else (z < dest)
-            follows = has_right if way == 0 else has_left
-            between()
-
-            @pl.when(passes)
-            def _():
-                y_copy(p, dest).wait_recv()
-                here = own[dest, :, span] + y_in[dest, :, span].astype(F32)
-
-                @pl.when(follows)
-                def _():
-                    chain_copy(p, way, dest).wait_recv()
-                    out[dest, :, span] = (here + into[dest, :, span].astype(F32)).astype(BF16)
-
-                @pl.when(jnp.logical_not(follows))
-                def _():
-                    out[dest, :, span] = here.astype(BF16)
-
-                chain_copy(p, way, dest).start()
-
-    def chain_end(p):
-        span = spans[p]
-        y_copy(p, z).wait_recv()
-        grad_ref[:, span] = own[z, :, span] + y_in[z, :, span].astype(F32)
-
-        @pl.when(has_left)
-        def _():
-            chain_copy(p, 1, z).wait_recv()
-            grad_ref[:, span] += right_in[z, :, span].astype(F32)
-
-        @pl.when(has_right)
-        def _():
-            chain_copy(p, 0, z).wait_recv()
-            grad_ref[:, span] += left_in[z, :, span].astype(F32)
-
-    tiles = iter(range(local // tile))
-
-    def between():
-        j = next(tiles, None)
-        if j is not None:
-            token_tile(j)
-
-    chain(0, lambda: None)
-    chain(1, between)
-    for j in tiles:
+    tiles = local // tile
+    for g in (0, 3, 1, 2):
+        y_phase(g)
+    own_phase(0)
+    chain(0)
+    own_phase(3)
+    gp_arrived(groups)
+    for j in range(tiles // 2):
         token_tile(j)
+    chain(3)
     chain_end(0)
-    chain_end(1)
+    own_phase(1)
+    for j in range(tiles // 2, tiles):
+        token_tile(j)
+    chain(1)
+    own_phase(2)
+    gain_sum = chain_end(3)
+    chain(2)
+    gain_sum += chain_end(1)
+    gain_sum += chain_end(2)
+    gain_pad[...] = jnp.zeros_like(gain_pad)
+    gain_pad[0:depth, :] = gain_sum / gain_t[mine, :]
+    ggain_ref[...] = gain_pad[...].T[0:1, 0:depth]
 
     gather_sent()
     for k in range(1, 4):
@@ -483,14 +500,13 @@
     for g in range(groups):
         core_copy(g).wait_send()
         x_copy(g).wait_send()
-    for k in range(3):
+    for k in range(groups + 1):
         gp_copy(k).wait_send()
-    for p in range(2):
-        for shard_z in range(nz):
-            y_copy(p, shard_z).wait_send()
-        for way, dest in steps:
-            passes = (z > dest) if way == 0 else (z < dest)
-            pl.when(passes)(lambda: chain_copy(p, way, dest).wait_send())
+    for g in range(groups):
+        for k in range(nz):
+            y_copy(g, k).wait_send()
+            pl.when(z > k)(lambda: chain_copy(g, 0, k).wait_send())
+            pl.when(z < k)(lambda: chain_copy(g, 1, k).wait_send())
 
 
 def fused(nz, width, tokens, grad_out, gain, qkv_weight, out_weight):
@@ -500,6 +516,7 @@
     half = rows // 2
     n = 2 * nz
     vmem = pl.BlockSpec(memory_space=pltpu.VMEM)
+    hbm = pl.BlockSpec(memory_space=pl.ANY)
     dma = pltpu.SemaphoreType.DMA
     exchange = pltpu.VMEM((4, half + 8, head), F32)
     pieces = pltpu.VMEM((nz, depth, 4 * head), BF16)
@@ -508,14 +525,19 @@
         out_shape=(
             jax.ShapeDtypeStruct((rows, local), BF16),
             jax.ShapeDtypeStruct((depth, 4 * head), F32),
+            jax.ShapeDtypeStruct((1, depth), F32),
         ),
-        in_specs=[vmem] * 5,
-        out_specs=(vmem, vmem),
+        in_specs=[hbm, hbm, vmem, hbm, hbm],
+        out_specs=(vmem, vmem, vmem),
         scratch_shapes=[
+            pltpu.VMEM((rows, local), BF16),
+            pltpu.VMEM((rows, local), BF16),
             pltpu.VMEM((4, local, head), BF16),
             pltpu.VMEM((rows, local), BF16),
             pltpu.VMEM((local, rows), BF16),
             pltpu.VMEM((local, rows), BF16),
+            pltpu.VMEM((local, 128), F32),
+            pltpu.VMEM((-(-depth // 128) * 128, 128), F32),
             pltpu.VMEM((4, 8, rows), F32),
             pltpu.VMEM((rows, 128), F32),
             exchange,
@@ -529,10 +551,9 @@
             pieces,
             pieces,
             pltpu.VMEM((nz, depth, 4 * head), F32),
-            pieces,
-            pieces,
-            pieces,
-            pieces,
+            pltpu.VMEM((2, nz, depth, 4 * head), BF16),
+            pltpu.VMEM((2, nz, depth, 4 * head), BF16),
+            dma((6,)),
             dma((4, 3, nz)),
             dma((4, n)),
             dma((4,)),
@@ -541,15 +562,15 @@
             dma((4,)),
             dma((4,)),
             dma((4,)),
-            dma((3,)),
-            dma((3,)),
-            dma((2, nz)),
-            dma((2, nz)),
-            dma((2, 2, nz)),
-            dma((2, 2, nz)),
+            dma((5,)),
+            dma((5,)),
+            dma((4, nz)),
+            dma((4, nz)),
+            dma((4, 2, nz)),
+            dma((4, 2, nz)),
         ],
         compiler_params=pltpu.CompilerParams(
-            collective_id=0, has_side_effects=True, vmem_limit_bytes=48 * 1024 * 1024
+            collective_id=0, has_side_effects=True, vmem_limit_bytes=58 * 1024 * 1024
         ),
         name="head_backward",
     )(tokens, grad_out, gain.reshape(1, local), qkv_weight, out_weight.T)
@@ -563,14 +584,10 @@
     depth = qkv_weight.shape[0]
     if depth % 64 or tok_rows != 2 * PATCHES or lax.axis_size("sec") != 4 or shards % 2:
         return by_collectives(tokens, grad_out, gain, qkv_weight, out_weight)
-    grad_tokens, grads = fused(
+    grad_tokens, grads, grad_gain = fused(
         shards // 2, model_width, tokens, grad_out, gain, qkv_weight, out_weight
     )
-    grad_qkv = grads[:, head_size:]
-    grad_outw = grads[:, :head_size].T
-    own_gain = lax.dynamic_slice_in_dim(gain, lax.axis_index("fsdp") * depth, depth)
-    grad_gain = jnp.sum(qkv_weight.astype(F32) * grad_qkv, axis=1) / own_gain
-    return grad_tokens, grad_qkv, grad_outw, grad_gain
+    return grad_tokens, grads[:, head_size:], grads[:, :head_size].T, grad_gain.reshape(depth)
 
 
 def by_collectives(tokens, grad_out, gain, qkv_weight, out_weight):

time: 85.3 us -> 79.8 us (0.936)
  Pallas kernels: 74.9 us -> 71.1 us
  other arithmetic: 2.08 us -> 0 us
    pallas_call x1, Pallas kernels: 74.9 us -> 71.1 us  [fused(): pl.pallas_call(functools.partial(kernel, nz, width), out_shape=(jax.Shape...]
    unnamed x9 -> x4, local copies, waits for them, and re-layouts: 5.66 us -> 3.22 us
    slice x0 -> x1, local copies, waits for them, and re-layouts: none -> 1.69 us  [on_device(): grads[:, head_size:]]
    div x1 -> x0, other arithmetic: 1.34 us -> none  [on_device(): grad_gain = jnp.sum(qkv_weight.astype(F32) * grad_qkv, axis=1) / own_gain]
    transpose x1, local copies, waits for them, and re-layouts: 0.65 us -> 1.54 us  [on_device(): grads[:, :head_size]]
where the time goes in v2:
time: 79.8 us; the launch traced here: 79.5 us
  Pallas kernels  71.1 us (89%)
  local copies, waits for them, and re-layouts  7.75 us (10%)
    pallas_call x1, Pallas kernels, fused(): pl.pallas_call(functools.partial(kernel, nz, width), out_shape=(jax.Shape...  71.1 us
    unnamed x4, local copies, waits for them, and re-layouts  3.22 us
    slice x1, local copies, waits for them, and re-layouts, on_device(): grads[:, head_size:]  1.69 us

profile of v2, /device:TPU:0, one launch (start us, length us, event | category | flops | bytes accessed | tf_op | source)
XLA Modules:
  0.0 79.5 jit_solution(12776903119032872968)
XLA Ops:
  0.6 1.3 %reshape.14.gain_ref = f32[1,1536]{1,0:T(1,128)} reshape(f32[1536]{0:T(1024)} %param.7) | data formatting | bytes 12288 | tf_op jit(solution)/shard_map/reshape | solution.py:576
  1.9 71.1 %head_backward.1 = (bf16[512,1536]{1,0:T(8,128)(2,1)}, f32[192,512]{1,0:T(8,128)}, f32[1,192]{1,0:T(1,128)}) custom-call(bf16[512,1536]{1,0:T(8,128)(2,1)} %tok_hbm.1, bf16[512,1536]{1,0:T(8,128)(2,1)} %go_hbm.1, f32[1,1536]{1,0:T(1,128)} %reshape.14.gain_ref, bf16[192,384]{1,0:T(8,128)(2,1)} %qkv_hbm.1, bf16[192,128]{1,0:T(8,128)(2,1)} %bitcast.4), custom_call_target="tpu_custom_call" | custom-call | tf_op jit(solution)/shard_map/head_backward/pallas_call | solution.py:523
  73.0 1.5 %slice_bitcast_fusion = f32[128,192]{0,1:T(8,128)} fusion(f32[192,512]{1,0:T(8,128)} %get-tuple-element.8), kind=kLoop, calls=%fused_computation | loop fusion | bytes 196608 | tf_op jit(solution)/shard_map/transpose | solution.py:590
  74.6 1.7 %slice.6 = f32[192,384]{1,0:T(8,128)} slice(f32[192,512]{1,0:T(8,128)} %get-tuple-element.8), slice={[0:192], [128:512]} | slice | bytes 589824 | tf_op jit(solution)/shard_map/slice | solution.py:590
  76.3 0.0 copy-start
  76.3 2.7 %copy.11 = bf16[512,1536]{1,0:T(8,128)(2,1)} copy(bf16[512,1536]{1,0:T(8,128)(2,1)} %get-tuple-element.14) | data formatting | bytes 3145728
  78.9 0.0 copy-done
  78.9 0.6 copy.12
Async XLA Ops:
  76.3 2.7 %copy-start = (f32[1,192]{1,0:T(1,128)S(1)}, f32[1,192]{1,0:T(1,128)}, u32[]{:S(2)}) copy-start(f32[1,192]{1,0:T(1,128)} %get-tuple-element.9) | copy-start | bytes 2308

commit v3 on v2

--- a/solution.py
+++ b/solution.py
@@ -183,10 +183,10 @@
                 pl.when(has_right & (z >= shard_z))(lambda: go_right(g, shard_z).wait_send())
                 go_y(g, shard_z).wait_send()
 
-    loads[0].wait()
-    send_own(0)
     loads[1].wait()
     send_own(1)
+    loads[2].wait()
+    send_own(2)
     loads[4].wait()
 
     step = 64
@@ -211,10 +211,10 @@
     for k in range(1, 4):
         stat_copy(k).start()
 
-    forward(0)
-    loads[2].wait()
-    send_own(2)
+    forward(1)
     loads[3].wait()
+    send_own(3)
+    loads[0].wait()
     loads[5].wait()
 
     tstep = 256
@@ -230,10 +230,6 @@
 
             lax.fori_loop(0, local // tstep, body, 0)
 
-    turn(go_ref, go_t)
-    forward(1)
-    send_own(3)
-    gain_t[...] = jnp.broadcast_to(gain_ref[...], (128, local)).T
 
     gain_row = gain_ref[...]
     g_hi = gain_row.astype(BF16)
@@ -275,8 +271,6 @@
         second_out[g] = first_own[g] + first_in[g]
         x_copy(g).start()
 
-    gathered(0)
-    project(0, go_ref)
 
     for k in range(1, 4):
         sender = (s + k) % 4
@@ -300,19 +294,24 @@
 
     lax.fori_loop(0, rows // step, norm, 0)
 
-    across_start(0)
     forward(2)
+    send_own(0)
+    turn(go_ref, go_t)
     gathered(1)
     project(1, hidden)
     forward(3)
     across_start(1)
+    turn(hidden, hidden_t)
     gathered(2)
     project(2, hidden)
-    turn(hidden, hidden_t)
+    forward(0)
     across_start(2)
     gathered(3)
     project(3, hidden)
+    gain_t[...] = jnp.broadcast_to(gain_ref[...], (128, local)).T
     across_start(3)
+    gathered(0)
+    project(0, go_ref)
 
     def finish(g):
         x_copy(g).wait_recv()
@@ -320,13 +319,13 @@
         return sums[g, 0:half, :].astype(BF16)
 
     scale = 1.0 / head**0.5
-    grad_att = finish(0)
     query = finish(1)
     key = finish(2)
     scores = nt(query, key) * scale
     e = jnp.exp(scores - jnp.max(scores, axis=-1, keepdims=True))
     probs = e / jnp.sum(e, axis=-1, keepdims=True)
     probs_b = probs.astype(BF16)
+    across_start(0)
 
     def gp_piece(k, r):
         return moments.at[r, :] if k == groups else gp.at[r, pl.ds(k * head, head)]
@@ -345,9 +344,102 @@
         gp_copy(k).start()
         return rounded
 
-    grad_value = gp_put(3, tn(probs_b, grad_att))
     value = finish(3)
     gp_put(0, nn(probs_b, value))
+
+    def span(g):
+        return slice(g * head, (g + 1) * head)
+
+    def cols_of(g):
+        return pl.ds(g * head, head)
+
+    near = (z < nz // 2).astype(jnp.int32)
+
+    def far_end(way, k):
+        return way * (nz - 1 - k) + (1 - way) * k
+
+    def part(g, shard):
+        r = pl.ds(pl.multiple_of(shard * depth, depth), depth)
+        return nn((go_t if g == 0 else hidden_t)[r, :], gp[:, span(g)])
+
+    def y_copy(g, shard_z):
+        return copy_to(
+            y_out.at[shard_z, :, cols_of(g)],
+            y_in.at[shard_z, :, cols_of(g)],
+            y_send.at[g, shard_z],
+            y_recv.at[g, shard_z],
+            other_y,
+        )
+
+    def y_phase(g):
+        gp_arrived(g)
+        for k in range(nz):
+            shard_z = far_end(near, k)
+            y_out[shard_z, :, span(g)] = part(g, shard_z * 2 + 1 - y).astype(BF16)
+            y_copy(g, shard_z).start()
+
+    def own_phase(g):
+        for k in range(nz):
+            own[k, :, span(g)] = part(g, k * 2 + y)
+
+    def chain_copy(g, way, dest):
+        return copy_to(
+            chain_out.at[way, dest, :, cols_of(g)],
+            chain_in.at[way, dest, :, cols_of(g)],
+            chain_send.at[g, way, dest],
+            chain_recv.at[g, way, dest],
+            {"fsdp": f + 4 * way - 2},
+        )
+
+    def chain(g):
+        for way in (near, 1 - near):
+            follows = ((way == 1) & has_left) | ((way == 0) & has_right)
+            for k in range(nz - 1):
+                dest = far_end(way, k)
+                passes = ((way == 1) & (dest > z)) | ((way == 0) & (dest < z))
+
+                @pl.when(passes)
+                def _():
+                    y_copy(g, dest).wait_recv()
+                    here = own[dest, :, span(g)] + y_in[dest, :, span(g)].astype(F32)
+
+                    @pl.when(follows)
+                    def _():
+                        chain_copy(g, way, dest).wait_recv()
+                        chain_out[way, dest, :, span(g)] = (
+                            here + chain_in[way, dest, :, span(g)].astype(F32)
+                        ).astype(BF16)
+
+                    @pl.when(jnp.logical_not(follows))
+                    def _():
+                        chain_out[way, dest, :, span(g)] = here.astype(BF16)
+
+                    chain_copy(g, way, dest).start()
+
+    def chain_end(g):
+        y_copy(g, z).wait_recv()
+        grad_ref[:, span(g)] = own[z, :, span(g)] + y_in[z, :, span(g)].astype(F32)
+
+        @pl.when(has_left)
+        def _():
+            chain_copy(g, 1, z).wait_recv()
+            grad_ref[:, span(g)] += chain_in[1, z, :, span(g)].astype(F32)
+
+        @pl.when(has_right)
+        def _():
+            chain_copy(g, 0, z).wait_recv()
+            grad_ref[:, span(g)] += chain_in[0, z, :, span(g)].astype(F32)
+
+        if g == 0:
+            return 0.0
+        held = weights[g, mine, :].astype(F32)
+        return jnp.sum(held * grad_ref[:, span(g)], axis=1, keepdims=True)
+
+    y_phase(0)
+    own_phase(0)
+
+    grad_att = finish(0)
+    grad_value = gp_put(3, tn(probs_b, grad_att))
     grad_prob = nt(grad_att, value)
     grad_score = (
         probs * (grad_prob - jnp.sum(grad_prob * probs, axis=-1, keepdims=True)) * scale
@@ -365,94 +457,6 @@
     moments[my_rows, :] = jnp.where(lane_h == 0, first, second) / width
     gp_copy(groups).start()
 
-    def span(g):
-        return slice(g * head, (g + 1) * head)
-
-    def cols_of(g):
-        return pl.ds(g * head, head)
-
-    near = (z < nz // 2).astype(jnp.int32)
-
-    def far_end(way, k):
-        return way * (nz - 1 - k) + (1 - way) * k
-
-    def part(g, shard):
-        r = pl.ds(pl.multiple_of(shard * depth, depth), depth)
-        return nn((go_t if g == 0 else hidden_t)[r, :], gp[:, span(g)])
-
-    def y_copy(g, shard_z):
-        return copy_to(
-            y_out.at[shard_z, :, cols_of(g)],
-            y_in.at[shard_z, :, cols_of(g)],
-            y_send.at[g, shard_z],
-            y_recv.at[g, shard_z],
-            other_y,
-        )
-
-    def y_phase(g):
-        gp_arrived(g)
-        for k in range(nz):
-            shard_z = far_end(near, k)
-            y_out[shard_z, :, span(g)] = part(g, shard_z * 2 + 1 - y).astype(BF16)
-            y_copy(g, shard_z).start()
-
-    def own_phase(g):
-        for k in range(nz):
-            own[k, :, span(g)] = part(g, k * 2 + y)
-
-    def chain_copy(g, way, dest):
-        return copy_to(
-            chain_out.at[way, dest, :, cols_of(g)],
-            chain_in.at[way, dest, :, cols_of(g)],
-            chain_send.at[g, way, dest],
-            chain_recv.at[g, way, dest],
-            {"fsdp": f + 4 * way - 2},
-        )
-
-    def chain(g):
-        for way in (near, 1 - near):
-            follows = ((way == 1) & has_left) | ((way == 0) & has_right)
-            for k in range(nz - 1):
-                dest = far_end(way, k)
-                passes = ((way == 1) & (dest > z)) | ((way == 0) & (dest < z))
-
-                @pl.when(passes)
-                def _():
-                    y_copy(g, dest).wait_recv()
-                    here = own[dest, :, span(g)] + y_in[dest, :, span(g)].astype(F32)
-
-                    @pl.when(follows)
-                    def _():
-                        chain_copy(g, way, dest).wait_recv()
-                        chain_out[way, dest, :, span(g)] = (
-                            here + chain_in[way, dest, :, span(g)].astype(F32)
-                        ).astype(BF16)
-
-                    @pl.when(jnp.logical_not(follows))
-                    def _():
-                        chain_out[way, dest, :, span(g)] = here.astype(BF16)
-
-                    chain_copy(g, way, dest).start()
-
-    def chain_end(g):
-        y_copy(g, z).wait_recv()
-        grad_ref[:, span(g)] = own[z, :, span(g)] + y_in[z, :, span(g)].astype(F32)
-
-        @pl.when(has_left)
-        def _():
-            chain_copy(g, 1, z).wait_recv()
-            grad_ref[:, span(g)] += chain_in[1, z, :, span(g)].astype(F32)
-
-        @pl.when(has_right)
-        def _():
-            chain_copy(g, 0, z).wait_recv()
-            grad_ref[:, span(g)] += chain_in[0, z, :, span(g)].astype(F32)
-
-        if g == 0:
-            return 0.0
-        held = weights[g, mine, :].astype(F32)
-        return jnp.sum(held * grad_ref[:, span(g)], axis=1, keepdims=True)
-
     tile = 256
 
     def token_tile(j):
@@ -471,9 +475,8 @@
         ).astype(BF16)
 
     tiles = local // tile
-    for g in (0, 3, 1, 2):
+    for g in (3, 1, 2):
         y_phase(g)
-    own_phase(0)
     chain(0)
     own_phase(3)
     gp_arrived(groups)
@@ -516,7 +519,7 @@
     half = rows // 2
     n = 2 * nz
     vmem = pl.BlockSpec(memory_space=pltpu.VMEM)
-    hbm = pl.BlockSpec(memory_space=pl.ANY)
+    hbm = pl.BlockSpec(memory_space=pltpu.HBM)
     dma = pltpu.SemaphoreType.DMA
     exchange = pltpu.VMEM((4, half + 8, head), F32)
     pieces = pltpu.VMEM((nz, depth, 4 * head), BF16)
@@ -570,7 +573,7 @@
             dma((4, 2, nz)),
         ],
         compiler_params=pltpu.CompilerParams(
-            collective_id=0, has_side_effects=True, vmem_limit_bytes=58 * 1024 * 1024
+            collective_id=0, has_side_effects=True, vmem_limit_bytes=52 * 1024 * 1024
         ),
         name="head_backward",
     )(tokens, grad_out, gain.reshape(1, local), qkv_weight, out_weight.T)

time: 79.8 us -> 78 us (0.977)
  Pallas kernels: 71.1 us -> 70.1 us
    unnamed x4 -> x6, local copies, waits for them, and re-layouts: 3.22 us -> 4.92 us
    pallas_call x1, Pallas kernels: 71.1 us -> 70.1 us  [fused(): pl.pallas_call(functools.partial(kernel, nz, width), out_shape=(jax.Shape...]
    slice x1, local copies, waits for them, and re-layouts: 1.69 us -> 0.74 us  [on_device(): grads[:, head_size:]]
    transpose x1, local copies, waits for them, and re-layouts: 1.54 us -> 0.65 us  [on_device(): grads[:, :head_size]]
where the time goes in v3:
time: 78 us; the launch traced here: 77.8 us
  Pallas kernels  70.1 us (90%)
  local copies, waits for them, and re-layouts  7.02 us (9%)
    pallas_call x1, Pallas kernels, fused(): pl.pallas_call(functools.partial(kernel, nz, width), out_shape=(jax.Shape...  70.1 us
    unnamed x6, local copies, waits for them, and re-layouts  4.92 us

profile of v3, /device:TPU:0, one launch (start us, length us, event | category | flops | bytes accessed | tf_op | source)
XLA Modules:
  0.0 77.8 jit_solution(4627702395457495284)
XLA Ops:
  0.6 0.7 reshape.14.gain_ref
  1.3 0.0 copy-start
  1.3 0.9 %copy-done = bf16[192,384]{1,0:T(8,128)(2,1)S(1)} copy-done((bf16[192,384]{1,0:T(8,128)(2,1)S(1)}, bf16[192,384]{1,0:T(8,128)(2,1)}, u32[]{:S(2)}) %copy-start) | copy-done | bytes 147480
  2.2 0.0 copy-start.1
  2.2 0.8 %copy-done.1 = bf16[128,192]{0,1:T(8,128)(2,1)S(1)} copy-done((bf16[128,192]{0,1:T(8,128)(2,1)S(1)}, bf16[128,192]{0,1:T(8,128)(2,1)}, u32[]{:S(2)}) %copy-start.1) | copy-done | bytes 49176
  3.0 70.1 %head_backward.1 = (bf16[512,1536]{1,0:T(8,128)(2,1)}, f32[192,512]{1,0:T(8,128)S(1)}, f32[1,192]{1,0:T(1,128)S(1)}) custom-call(bf16[512,1536]{1,0:T(8,128)(2,1)} %tok_hbm.1, bf16[512,1536]{1,0:T(8,128)(2,1)} %go_hbm.1, f32[1,1536]{1,0:T(1,128)S(1)} %reshape.14.gain_ref, bf16[192,384]{1,0:T(8,128)(2,1)S(1)} %copy-done, bf16[192,128]{1,0:T(8,128)(2,1)S(1)} %bitcast.4), custom_call_target="tpu_custom_call" | custom-call | tf_op jit(solution)/shard_map/head_backward/pallas_call | solution.py:526
  73.2 0.7 slice_bitcast_fusion
  73.8 0.7 slice.6
  74.6 2.7 %copy.11 = bf16[512,1536]{1,0:T(8,128)(2,1)} copy(bf16[512,1536]{1,0:T(8,128)(2,1)} %get-tuple-element.14) | data formatting | bytes 3145728
  77.2 0.6 copy.12
Async XLA Ops:
  1.3 0.9 %copy-start = (bf16[192,384]{1,0:T(8,128)(2,1)S(1)}, bf16[192,384]{1,0:T(8,128)(2,1)}, u32[]{:S(2)}) copy-start(bf16[192,384]{1,0:T(8,128)(2,1)} %qkv_hbm.1) | copy-start | bytes 442372
  2.2 0.8 %copy-start.1 = (bf16[128,192]{0,1:T(8,128)(2,1)S(1)}, bf16[128,192]{0,1:T(8,128)(2,1)}, u32[]{:S(2)}) copy-start(bf16[128,192]{0,1:T(8,128)(2,1)} %param.9) | copy-start | bytes 147460

commit v4 on v3

--- a/solution.py
+++ b/solution.py
@@ -157,20 +157,25 @@
         pl.when(has_right)(lambda: go_right(g, z).start())
         go_y(g, z).start()
 
-    def forward(g):
-        for d in range(1, nz):
-
-            @pl.when(z - d >= 0)
-            def _():
-                arrived(g, (z - d) * 2 + y)
-                pl.when(has_right)(lambda: go_right(g, z - d).start())
-                go_y(g, z - d).start()
-
-            @pl.when(z + d < nz)
-            def _():
-                arrived(g, (z + d) * 2 + y)
-                pl.when(has_left)(lambda: go_left(g, z + d).start())
-                go_y(g, z + d).start()
+    def forward(g, d):
+        @pl.when(z - d >= 0)
+        def _():
+            arrived(g, (z - d) * 2 + y)
+            pl.when(has_right)(lambda: go_right(g, z - d).start())
+            go_y(g, z - d).start()
+
+        @pl.when(z + d < nz)
+        def _():
+            arrived(g, (z + d) * 2 + y)
+            pl.when(has_left)(lambda: go_left(g, z + d).start())
+            go_y(g, z + d).start()
+
+    turn_order = (1, 2, 3, 0)
+
+    def wave(w):
+        for g_at, g in enumerate(turn_order):
+            if 1 <= w - g_at < nz:
+                forward(g, w - g_at)
 
     def gathered(g):
         for shard_z in range(nz):
@@ -211,10 +216,13 @@
     for k in range(1, 4):
         stat_copy(k).start()
 
-    forward(1)
+    wave(1)
     loads[3].wait()
     send_own(3)
+    wave(2)
     loads[0].wait()
+    send_own(0)
+    wave(3)
     loads[5].wait()
 
     tstep = 256
@@ -294,22 +302,22 @@
 
     lax.fori_loop(0, rows // step, norm, 0)
 
-    forward(2)
-    send_own(0)
-    turn(go_ref, go_t)
+    wave(4)
     gathered(1)
     project(1, hidden)
-    forward(3)
+    wave(5)
     across_start(1)
-    turn(hidden, hidden_t)
+    for w in range(6, nz + len(turn_order) - 1):
+        wave(w)
     gathered(2)
     project(2, hidden)
-    forward(0)
+    turn(go_ref, go_t)
     across_start(2)
     gathered(3)
     project(3, hidden)
+    turn(hidden, hidden_t)
+    across_start(3)
     gain_t[...] = jnp.broadcast_to(gain_ref[...], (128, local)).T
-    across_start(3)
     gathered(0)
     project(0, go_ref)
 
@@ -391,30 +399,30 @@
             {"fsdp": f + 4 * way - 2},
         )
 
-    def chain(g):
-        for way in (near, 1 - near):
-            follows = ((way == 1) & has_left) | ((way == 0) & has_right)
-            for k in range(nz - 1):
-                dest = far_end(way, k)
-                passes = ((way == 1) & (dest > z)) | ((way == 0) & (dest < z))
-
-                @pl.when(passes)
+    def chain(g, leg):
+        way = near if leg == 0 else 1 - near
+        follows = ((way == 1) & has_left) | ((way == 0) & has_right)
+        for k in range(nz - 1):
+            dest = far_end(way, k)
+            passes = ((way == 1) & (dest > z)) | ((way == 0) & (dest < z))
+
+            @pl.when(passes)
+            def _():
+                y_copy(g, dest).wait_recv()
+                here = own[dest, :, span(g)] + y_in[dest, :, span(g)].astype(F32)
+
+                @pl.when(follows)
                 def _():
-                    y_copy(g, dest).wait_recv()
-                    here = own[dest, :, span(g)] + y_in[dest, :, span(g)].astype(F32)
-
-                    @pl.when(follows)
-                    def _():
-                        chain_copy(g, way, dest).wait_recv()
-                        chain_out[way, dest, :, span(g)] = (
-                            here + chain_in[way, dest, :, span(g)].astype(F32)
-                        ).astype(BF16)
-
-                    @pl.when(jnp.logical_not(follows))
-                    def _():
-                        chain_out[way, dest, :, span(g)] = here.astype(BF16)
-
-                    chain_copy(g, way, dest).start()
+                    chain_copy(g, way, dest).wait_recv()
+                    chain_out[way, dest, :, span(g)] = (
+                        here + chain_in[way, dest, :, span(g)].astype(F32)
+                    ).astype(BF16)
+
+                @pl.when(jnp.logical_not(follows))
+                def _():
+                    chain_out[way, dest, :, span(g)] = here.astype(BF16)
+
+                chain_copy(g, way, dest).start()
 
     def chain_end(g):
         y_copy(g, z).wait_recv()
@@ -477,20 +485,29 @@
     tiles = local // tile
     for g in (3, 1, 2):
         y_phase(g)
-    chain(0)
+    cuts = [tiles * k // 3 for k in range(4)]
+
+    def some_tiles(k):
+        for j in range(cuts[k], cuts[k + 1]):
+            token_tile(j)
+
+    chain(0, 0)
     own_phase(3)
+    chain(0, 1)
     gp_arrived(groups)
-    for j in range(tiles // 2):
-        token_tile(j)
-    chain(3)
+    some_tiles(0)
+    chain(3, 0)
+    own_phase(1)
     chain_end(0)
-    own_phase(1)
-    for j in range(tiles // 2, tiles):
-        token_tile(j)
-    chain(1)
+    some_tiles(1)
+    chain(1, 0)
+    chain(3, 1)
     own_phase(2)
     gain_sum = chain_end(3)
-    chain(2)
+    chain(2, 0)
+    chain(1, 1)
+    some_tiles(2)
+    chain(2, 1)
     gain_sum += chain_end(1)
     gain_sum += chain_end(2)
     gain_pad[...] = jnp.zeros_like(gain_pad)
@@ -573,7 +590,7 @@
             dma((4, 2, nz)),
         ],
         compiler_params=pltpu.CompilerParams(
-            collective_id=0, has_side_effects=True, vmem_limit_bytes=52 * 1024 * 1024
+            collective_id=0, has_side_effects=True, vmem_limit_bytes=50 * 1024 * 1024
         ),
         name="head_backward",
     )(tokens, grad_out, gain.reshape(1, local), qkv_weight, out_weight.T)

time: 78 us -> 75.7 us (0.971)
  Pallas kernels: 70.1 us -> 67.9 us
    pallas_call x1, Pallas kernels: 70.1 us -> 67.9 us  [fused(): pl.pallas_call(functools.partial(kernel, nz, width), out_shape=(jax.Shape...]
    unnamed x6 -> x8, local copies, waits for them, and re-layouts: 4.92 us -> 4.82 us
where the time goes in v4:
time: 75.7 us; the launch traced here: 75.4 us
  Pallas kernels  67.9 us (90%)
  local copies, waits for them, and re-layouts  6.91 us (9%)
    pallas_call x1, Pallas kernels, fused(): pl.pallas_call(functools.partial(kernel, nz, width), out_shape=(jax.Shape...  67.9 us
    unnamed x8, local copies, waits for them, and re-layouts  4.82 us

profile of v4, /device:TPU:0, one launch (start us, length us, event | category | flops | bytes accessed | tf_op | source)
XLA Modules:
  0.0 75.4 jit_solution(7246058642209611701)
XLA Ops:
  0.6 0.7 reshape.14.gain_ref
  1.3 0.0 copy-start
  1.3 1.4 %copy-done = bf16[512,1536]{1,0:T(8,128)(2,1)S(1)} copy-done((bf16[512,1536]{1,0:T(8,128)(2,1)S(1)}, bf16[512,1536]{1,0:T(8,128)(2,1)}, u32[]{:S(2)}) %copy-start) | copy-done | bytes 1572888
  2.7 0.0 copy-start.1
  2.7 0.9 %copy-done.1 = bf16[192,384]{1,0:T(8,128)(2,1)S(1)} copy-done((bf16[192,384]{1,0:T(8,128)(2,1)S(1)}, bf16[192,384]{1,0:T(8,128)(2,1)}, u32[]{:S(2)}) %copy-start.1) | copy-done | bytes 147480
  3.7 0.0 copy-start.2
  3.7 0.8 %copy-done.2 = bf16[128,192]{0,1:T(8,128)(2,1)S(1)} copy-done((bf16[128,192]{0,1:T(8,128)(2,1)S(1)}, bf16[128,192]{0,1:T(8,128)(2,1)}, u32[]{:S(2)}) %copy-start.2) | copy-done | bytes 49176
  4.5 67.9 %head_backward.1 = (bf16[512,1536]{1,0:T(8,128)(2,1)S(1)}, f32[192,512]{1,0:T(8,128)S(1)}, f32[1,192]{1,0:T(1,128)S(1)}) custom-call(bf16[512,1536]{1,0:T(8,128)(2,1)S(1)} %copy-done, bf16[512,1536]{1,0:T(8,128)(2,1)} %go_hbm.1, f32[1,1536]{1,0:T(1,128)S(1)} %reshape.14.gain_ref, bf16[192,384]{1,0:T(8,128)(2,1)S(1)} %copy-done.1, bf16[192,128]{1,0:T(8,128)(2,1)S(1)} %bitcast.4), custom_call_target="tpu_custom_call" | custom-call | tf_op jit(solution)/shard_map/head_backward/pallas_call | solution.py:543
  72.3 0.7 slice_bitcast_fusion
  73.0 0.7 slice.6
  73.7 1.1 %copy.11 = bf16[512,1536]{1,0:T(8,128)(2,1)} copy(bf16[512,1536]{1,0:T(8,128)(2,1)S(1)} %get-tuple-element.14) | data formatting | bytes 3145728
  74.8 0.6 copy.12
Async XLA Ops:
  1.3 1.4 %copy-start = (bf16[512,1536]{1,0:T(8,128)(2,1)S(1)}, bf16[512,1536]{1,0:T(8,128)(2,1)}, u32[]{:S(2)}) copy-start(bf16[512,1536]{1,0:T(8,128)(2,1)} %tok_hbm.1) | copy-start | bytes 4718596
  2.7 0.9 %copy-start.1 = (bf16[192,384]{1,0:T(8,128)(2,1)S(1)}, bf16[192,384]{1,0:T(8,128)(2,1)}, u32[]{:S(2)}) copy-start(bf16[192,384]{1,0:T(8,128)(2,1)} %qkv_hbm.1) | copy-start | bytes 442372
  3.7 0.8 %copy-start.2 = (bf16[128,192]{0,1:T(8,128)(2,1)S(1)}, bf16[128,192]{0,1:T(8,128)(2,1)}, u32[]{:S(2)}) copy-start(bf16[128,192]{0,1:T(8,128)(2,1)} %param.9) | copy-start | bytes 147460

commit v5 on v4

--- a/solution.py
+++ b/solution.py
@@ -63,6 +63,8 @@
     first_in,
     second_out,
     second_in,
+    att_out,
+    att_in,
     gp,
     moments,
     sums,
@@ -260,9 +262,8 @@
         )
 
     def x_copy(g):
-        return copy_to(
-            second_out.at[g], second_in.at[g], x_send.at[g], x_recv.at[g], across
-        )
+        src, dst = (att_out, att_in) if g == 0 else (second_out.at[g], second_in.at[g])
+        return copy_to(src, dst, x_send.at[g], x_recv.at[g], across)
 
     def project(g, left):
         w = weights[g]
@@ -276,7 +277,10 @@
 
     def across_start(g):
         core_copy(g).wait_recv()
-        second_out[g] = first_own[g] + first_in[g]
+        if g == 0:
+            att_out[...] = (first_own[g, 0:half, :] + first_in[g, 0:half, :]).astype(BF16)
+        else:
+            second_out[g] = first_own[g] + first_in[g]
         x_copy(g).start()
 
 
@@ -323,6 +327,8 @@
 
     def finish(g):
         x_copy(g).wait_recv()
+        if g == 0:
+            return (att_out[...].astype(F32) + att_in[...].astype(F32)).astype(BF16)
         sums[g] = second_out[g] + second_in[g]
         return sums[g, 0:half, :].astype(BF16)
 
@@ -336,7 +342,7 @@
     across_start(0)
 
     def gp_piece(k, r):
-        return moments.at[r, :] if k == groups else gp.at[r, pl.ds(k * head, head)]
+        return moments.at[r, :] if k == groups else gp.at[k, r, :]
 
     def gp_copy(k):
         ref = gp_piece(k, my_rows)
@@ -348,7 +354,7 @@
 
     def gp_put(k, result):
         rounded = result.astype(BF16)
-        gp[my_rows, k * head : (k + 1) * head] = rounded
+        gp[k, my_rows, :] = rounded
         gp_copy(k).start()
         return rounded
 
@@ -358,9 +364,6 @@
     def span(g):
         return slice(g * head, (g + 1) * head)
 
-    def cols_of(g):
-        return pl.ds(g * head, head)
-
     near = (z < nz // 2).astype(jnp.int32)
 
     def far_end(way, k):
@@ -368,12 +371,12 @@
 
     def part(g, shard):
         r = pl.ds(pl.multiple_of(shard * depth, depth), depth)
-        return nn((go_t if g == 0 else hidden_t)[r, :], gp[:, span(g)])
+        return nn((go_t if g == 0 else hidden_t)[r, :], gp[g])
 
     def y_copy(g, shard_z):
         return copy_to(
-            y_out.at[shard_z, :, cols_of(g)],
-            y_in.at[shard_z, :, cols_of(g)],
+            y_out.at[g, shard_z],
+            y_in.at[g, shard_z],
             y_send.at[g, shard_z],
             y_recv.at[g, shard_z],
             other_y,
@@ -383,17 +386,17 @@
         gp_arrived(g)
         for k in range(nz):
             shard_z = far_end(near, k)
-            y_out[shard_z, :, span(g)] = part(g, shard_z * 2 + 1 - y).astype(BF16)
+            y_out[g, shard_z] = part(g, shard_z * 2 + 1 - y).astype(BF16)
             y_copy(g, shard_z).start()
 
     def own_phase(g):
         for k in range(nz):
-            own[k, :, span(g)] = part(g, k * 2 + y)
+            own[g, k] = part(g, k * 2 + y)
 
     def chain_copy(g, way, dest):
         return copy_to(
-            chain_out.at[way, dest, :, cols_of(g)],
-            chain_in.at[way, dest, :, cols_of(g)],
+            chain_out.at[g, way, dest],
+            chain_in.at[g, way, dest],
             chain_send.at[g, way, dest],
             chain_recv.at[g, way, dest],
             {"fsdp": f + 4 * way - 2},
@@ -409,34 +412,34 @@
             @pl.when(passes)
             def _():
                 y_copy(g, dest).wait_recv()
-                here = own[dest, :, span(g)] + y_in[dest, :, span(g)].astype(F32)
+                here = own[g, dest] + y_in[g, dest].astype(F32)
 
                 @pl.when(follows)
                 def _():
                     chain_copy(g, way, dest).wait_recv()
-                    chain_out[way, dest, :, span(g)] = (
-                        here + chain_in[way, dest, :, span(g)].astype(F32)
+                    chain_out[g, way, dest] = (
+                        here + chain_in[g, way, dest].astype(F32)
                     ).astype(BF16)
 
                 @pl.when(jnp.logical_not(follows))
                 def _():
-                    chain_out[way, dest, :, span(g)] = here.astype(BF16)
+                    chain_out[g, way, dest] = here.astype(BF16)
 
                 chain_copy(g, way, dest).start()
 
     def chain_end(g):
         y_copy(g, z).wait_recv()
-        grad_ref[:, span(g)] = own[z, :, span(g)] + y_in[z, :, span(g)].astype(F32)
+        grad_ref[:, span(g)] = own[g, z] + y_in[g, z].astype(F32)
 
         @pl.when(has_left)
         def _():
             chain_copy(g, 1, z).wait_recv()
-            grad_ref[:, span(g)] += chain_in[1, z, :, span(g)].astype(F32)
+            grad_ref[:, span(g)] += chain_in[g, 1, z].astype(F32)
 
         @pl.when(has_right)
         def _():
             chain_copy(g, 0, z).wait_recv()
-            grad_ref[:, span(g)] += chain_in[0, z, :, span(g)].astype(F32)
+            grad_ref[:, span(g)] += chain_in[g, 0, z].astype(F32)
 
         if g == 0:
             return 0.0
@@ -444,7 +447,6 @@
         return jnp.sum(held * grad_ref[:, span(g)], axis=1, keepdims=True)
 
     y_phase(0)
-    own_phase(0)
 
     grad_att = finish(0)
     grad_value = gp_put(3, tn(probs_b, grad_att))
@@ -469,9 +471,9 @@
 
     def token_tile(j):
         cols = pl.ds(pl.multiple_of(j * tile, tile), tile)
-        grad_hidden = nt(gp[:, head : 2 * head], weights[1, cols, :])
+        grad_hidden = nt(gp[1], weights[1, cols, :])
         for g in range(2, groups):
-            grad_hidden += nt(gp[:, g * head : (g + 1) * head], weights[g, cols, :])
+            grad_hidden += nt(gp[g], weights[g, cols, :])
         m = mean_inv[...]
         inv = m[:, 1:2]
         normed = (tok_ref[:, cols].astype(F32) - m[:, 0:1]) * inv
@@ -491,6 +493,7 @@
         for j in range(cuts[k], cuts[k + 1]):
             token_tile(j)
 
+    own_phase(0)
     chain(0, 0)
     own_phase(3)
     chain(0, 1)
@@ -539,7 +542,7 @@
     hbm = pl.BlockSpec(memory_space=pltpu.HBM)
     dma = pltpu.SemaphoreType.DMA
     exchange = pltpu.VMEM((4, half + 8, head), F32)
-    pieces = pltpu.VMEM((nz, depth, 4 * head), BF16)
+    pieces = pltpu.VMEM((4, nz, depth, head), BF16)
     return pl.pallas_call(
         functools.partial(kernel, nz, width),
         out_shape=(
@@ -565,14 +568,16 @@
             exchange,
             exchange,
             exchange,
-            pltpu.VMEM((rows, 4 * head), BF16),
+            pltpu.VMEM((half, head), BF16),
+            pltpu.VMEM((half, head), BF16),
+            pltpu.VMEM((4, rows, head), BF16),
             pltpu.VMEM((rows, 128), F32),
             exchange,
             pieces,
             pieces,
-            pltpu.VMEM((nz, depth, 4 * head), F32),
-            pltpu.VMEM((2, nz, depth, 4 * head), BF16),
-            pltpu.VMEM((2, nz, depth, 4 * head), BF16),
+            pltpu.VMEM((4, nz, depth, head), F32),
+            pltpu.VMEM((4, 2, nz, depth, head), BF16),
+            pltpu.VMEM((4, 2, nz, depth, head), BF16),
             dma((6,)),
             dma((4, 3, nz)),
             dma((4, n)),

time: 75.7 us -> 75.5 us (level)
  no operation moved by 1% of the time
where the time goes in v5:
time: 75.5 us; the launch traced here: 75.2 us
  Pallas kernels  67.6 us (90%)
  local copies, waits for them, and re-layouts  6.91 us (9%)
    pallas_call x1, Pallas kernels, fused(): pl.pallas_call(functools.partial(kernel, nz, width), out_shape=(jax.Shape...  67.6 us
    unnamed x8, local copies, waits for them, and re-layouts  4.82 us

profile of v5, /device:TPU:0, one launch (start us, length us, event | category | flops | bytes accessed | tf_op | source)
XLA Modules:
  0.0 75.2 jit_solution(14670039771170786550)
XLA Ops:
  0.6 0.7 reshape.14.gain_ref
  1.3 0.0 copy-start
  1.3 1.4 %copy-done = bf16[512,1536]{1,0:T(8,128)(2,1)S(1)} copy-done((bf16[512,1536]{1,0:T(8,128)(2,1)S(1)}, bf16[512,1536]{1,0:T(8,128)(2,1)}, u32[]{:S(2)}) %copy-start) | copy-done | bytes 1572888
  2.7 0.0 copy-start.1
  2.7 0.9 %copy-done.1 = bf16[192,384]{1,0:T(8,128)(2,1)S(1)} copy-done((bf16[192,384]{1,0:T(8,128)(2,1)S(1)}, bf16[192,384]{1,0:T(8,128)(2,1)}, u32[]{:S(2)}) %copy-start.1) | copy-done | bytes 147480
  3.7 0.0 copy-start.2
  3.7 0.8 %copy-done.2 = bf16[128,192]{0,1:T(8,128)(2,1)S(1)} copy-done((bf16[128,192]{0,1:T(8,128)(2,1)S(1)}, bf16[128,192]{0,1:T(8,128)(2,1)}, u32[]{:S(2)}) %copy-start.2) | copy-done | bytes 49176
  4.5 67.6 %head_backward.1 = (bf16[512,1536]{1,0:T(8,128)(2,1)S(1)}, f32[192,512]{1,0:T(8,128)S(1)}, f32[1,192]{1,0:T(1,128)S(1)}) custom-call(bf16[512,1536]{1,0:T(8,128)(2,1)S(1)} %copy-done, bf16[512,1536]{1,0:T(8,128)(2,1)} %go_hbm.1, f32[1,1536]{1,0:T(1,128)S(1)} %reshape.14.gain_ref, bf16[192,384]{1,0:T(8,128)(2,1)S(1)} %copy-done.1, bf16[192,128]{1,0:T(8,128)(2,1)S(1)} %bitcast.4), custom_call_target="tpu_custom_call" | custom-call | tf_op jit(solution)/shard_map/head_backward/pallas_call | solution.py:546
  72.1 0.7 slice_bitcast_fusion
  72.8 0.7 slice.6
  73.5 1.1 %copy.11 = bf16[512,1536]{1,0:T(8,128)(2,1)} copy(bf16[512,1536]{1,0:T(8,128)(2,1)S(1)} %get-tuple-element.14) | data formatting | bytes 3145728
  74.6 0.6 copy.12
Async XLA Ops:
  1.3 1.4 %copy-start = (bf16[512,1536]{1,0:T(8,128)(2,1)S(1)}, bf16[512,1536]{1,0:T(8,128)(2,1)}, u32[]{:S(2)}) copy-start(bf16[512,1536]{1,0:T(8,128)(2,1)} %tok_hbm.1) | copy-start | bytes 4718596
  2.7 0.9 %copy-start.1 = (bf16[192,384]{1,0:T(8,128)(2,1)S(1)}, bf16[192,384]{1,0:T(8,128)(2,1)}, u32[]{:S(2)}) copy-start(bf16[192,384]{1,0:T(8,128)(2,1)} %qkv_hbm.1) | copy-start | bytes 442372
  3.7 0.8 %copy-start.2 = (bf16[128,192]{0,1:T(8,128)(2,1)S(1)}, bf16[128,192]{0,1:T(8,128)(2,1)}, u32[]{:S(2)}) copy-start(bf16[128,192]{0,1:T(8,128)(2,1)} %param.9) | copy-start | bytes 147460

commit v6 on v5

--- a/solution.py
+++ b/solution.py
@@ -63,8 +63,6 @@
     first_in,
     second_out,
     second_in,
-    att_out,
-    att_in,
     gp,
     moments,
     sums,
@@ -262,8 +260,9 @@
         )
 
     def x_copy(g):
-        src, dst = (att_out, att_in) if g == 0 else (second_out.at[g], second_in.at[g])
-        return copy_to(src, dst, x_send.at[g], x_recv.at[g], across)
+        return copy_to(
+            second_out.at[g], second_in.at[g], x_send.at[g], x_recv.at[g], across
+        )
 
     def project(g, left):
         w = weights[g]
@@ -277,10 +276,7 @@
 
     def across_start(g):
         core_copy(g).wait_recv()
-        if g == 0:
-            att_out[...] = (first_own[g, 0:half, :] + first_in[g, 0:half, :]).astype(BF16)
-        else:
-            second_out[g] = first_own[g] + first_in[g]
+        second_out[g] = first_own[g] + first_in[g]
         x_copy(g).start()
 
 
@@ -327,8 +323,6 @@
 
     def finish(g):
         x_copy(g).wait_recv()
-        if g == 0:
-            return (att_out[...].astype(F32) + att_in[...].astype(F32)).astype(BF16)
         sums[g] = second_out[g] + second_in[g]
         return sums[g, 0:half, :].astype(BF16)
 
@@ -454,6 +448,7 @@
     grad_score = (
         probs * (grad_prob - jnp.sum(grad_prob * probs, axis=-1, keepdims=True)) * scale
     ).astype(BF16)
+    y_phase(3)
     grad_query = gp_put(1, nn(grad_score, key))
     grad_key = gp_put(2, tn(grad_score, query))
     lane_h = lax.broadcasted_iota(jnp.int32, (half, 128), 1)
@@ -485,8 +480,8 @@
         ).astype(BF16)
 
     tiles = local // tile
-    for g in (3, 1, 2):
-        y_phase(g)
+    y_phase(1)
+    y_phase(2)
     cuts = [tiles * k // 3 for k in range(4)]
 
     def some_tiles(k):
@@ -568,8 +563,6 @@
             exchange,
             exchange,
             exchange,
-            pltpu.VMEM((half, head), BF16),
-            pltpu.VMEM((half, head), BF16),
             pltpu.VMEM((4, rows, head), BF16),
             pltpu.VMEM((rows, 128), F32),
             exchange,

time: 75.5 us -> 76.7 us (1.016)
  Pallas kernels: 67.6 us -> 68.9 us
    pallas_call x1, Pallas kernels: 67.6 us -> 68.9 us  [fused(): pl.pallas_call(functools.partial(kernel, nz, width), out_shape=(jax.Shape...]
where the time goes in v6:
time: 76.7 us; the launch traced here: 76.5 us
  Pallas kernels  68.9 us (90%)
  local copies, waits for them, and re-layouts  6.91 us (9%)
    pallas_call x1, Pallas kernels, fused(): pl.pallas_call(functools.partial(kernel, nz, width), out_shape=(jax.Shape...  68.9 us
    unnamed x8, local copies, waits for them, and re-layouts  4.82 us

profile of v6, /device:TPU:0, one launch (start us, length us, event | category | flops | bytes accessed | tf_op | source)
XLA Modules:
  0.0 76.5 jit_solution(2196403630087091009)
XLA Ops:
  0.6 0.7 reshape.14.gain_ref
  1.3 0.0 copy-start
  1.3 1.4 %copy-done = bf16[512,1536]{1,0:T(8,128)(2,1)S(1)} copy-done((bf16[512,1536]{1,0:T(8,128)(2,1)S(1)}, bf16[512,1536]{1,0:T(8,128)(2,1)}, u32[]{:S(2)}) %copy-start) | copy-done | bytes 1572888
  2.7 0.0 copy-start.1
  2.7 0.9 %copy-done.1 = bf16[192,384]{1,0:T(8,128)(2,1)S(1)} copy-done((bf16[192,384]{1,0:T(8,128)(2,1)S(1)}, bf16[192,384]{1,0:T(8,128)(2,1)}, u32[]{:S(2)}) %copy-start.1) | copy-done | bytes 147480
  3.7 0.0 copy-start.2
  3.7 0.8 %copy-done.2 = bf16[128,192]{0,1:T(8,128)(2,1)S(1)} copy-done((bf16[128,192]{0,1:T(8,128)(2,1)S(1)}, bf16[128,192]{0,1:T(8,128)(2,1)}, u32[]{:S(2)}) %copy-start.2) | copy-done | bytes 49176
  4.5 68.9 %head_backward.1 = (bf16[512,1536]{1,0:T(8,128)(2,1)S(1)}, f32[192,512]{1,0:T(8,128)S(1)}, f32[1,192]{1,0:T(1,128)S(1)}) custom-call(bf16[512,1536]{1,0:T(8,128)(2,1)S(1)} %copy-done, bf16[512,1536]{1,0:T(8,128)(2,1)} %go_hbm.1, f32[1,1536]{1,0:T(1,128)S(1)} %reshape.14.gain_ref, bf16[192,384]{1,0:T(8,128)(2,1)S(1)} %copy-done.1, bf16[192,128]{1,0:T(8,128)(2,1)S(1)} %bitcast.4), custom_call_target="tpu_custom_call" | custom-call | tf_op jit(solution)/shard_map/head_backward/pallas_call | solution.py:541
  73.4 0.7 slice_bitcast_fusion
  74.0 0.7 slice.6
  74.8 1.1 %copy.11 = bf16[512,1536]{1,0:T(8,128)(2,1)} copy(bf16[512,1536]{1,0:T(8,128)(2,1)S(1)} %get-tuple-element.14) | data formatting | bytes 3145728
  75.9 0.6 copy.12
Async XLA Ops:
  1.3 1.4 %copy-start = (bf16[512,1536]{1,0:T(8,128)(2,1)S(1)}, bf16[512,1536]{1,0:T(8,128)(2,1)}, u32[]{:S(2)}) copy-start(bf16[512,1536]{1,0:T(8,128)(2,1)} %tok_hbm.1) | copy-start | bytes 4718596
  2.7 0.9 %copy-start.1 = (bf16[192,384]{1,0:T(8,128)(2,1)S(1)}, bf16[192,384]{1,0:T(8,128)(2,1)}, u32[]{:S(2)}) copy-start(bf16[192,384]{1,0:T(8,128)(2,1)} %qkv_hbm.1) | copy-start | bytes 442372
  3.7 0.8 %copy-start.2 = (bf16[128,192]{0,1:T(8,128)(2,1)S(1)}, bf16[128,192]{0,1:T(8,128)(2,1)}, u32[]{:S(2)}) copy-start(bf16[128,192]{0,1:T(8,128)(2,1)} %param.9) | copy-start | bytes 147460
